TPU v7x, 512 devices: a whole 4x4x16 slice. The times are simulated.
512 devices in a mesh: inst: 32 (over z_lo, y), tp: 16 (over x, z_hi, core).
Axes of the slice: x: 4, y: 4, z: 16 (z_hi: 2, z_lo: 8; z = z_hi * 8 + z_lo), core: 2. Of those that a mesh axis runs over, the one named last changes fastest.
Arguments:
- x_one: bfloat16 [96, 8192], P('inst', 'tp'), may hold values from -6 to 6
- z_one: bfloat16 [96, 8192], P('inst', 'tp'), may hold values from -6 to 6
- dt_one: bfloat16 [96, 128], P('inst', 'tp'), may hold values from -6 to 6
- b_one: bfloat16 [96, 1024], P('inst'), may hold values from -6 to 6
- c_one: bfloat16 [96, 1024], P('inst'), may hold values from -0.625 to 0.625
- q_one: bfloat16 [96, 8192], P('inst')
- kv_one: bfloat16 [96, 2048], P('inst'), may hold values from -6 to 6
- state: float32 [96, 128, 64, 256], P('inst', 'tp'), may hold values from -6 to 6
- cache: bfloat16 [384, 16, 32768], P('inst', None, 'tp'), may hold values from -6 to 6
- page_table: int32 [96, 64], P('inst', 'tp'), may hold values from 0 to 11, as said below
- lengths: int32 [96], replicated, may hold values from 1 to 1022, as said below
- migration: int32 [32, 2], replicated, may hold values from 0 to 95, as said below
- decay_rate: float32 [128], P('tp'), may hold values from 0.02 to 8
- dt_bias: float32 [128], P('tp'), may hold values from -1 to 1
- skip_gain: float32 [128], P('tp'), may hold values from 0.5 to 1.5
- norm_gain: float32 [8192], P('tp'), may hold values from 0.5 to 1.5
- x_two: bfloat16 [96, 8192], P('inst', 'tp'), may hold values from -6 to 6
- z_two: bfloat16 [96, 8192], P('inst', 'tp'), may hold values from -6 to 6
- dt_two: bfloat16 [96, 128], P('inst', 'tp'), may hold values from -6 to 6
- b_two: bfloat16 [96, 1024], P('inst'), may hold values from -6 to 6
- c_two: bfloat16 [96, 1024], P('inst'), may hold values from -0.625 to 0.625
- q_two: bfloat16 [96, 8192], P('inst')
- kv_two: bfloat16 [96, 2048], P('inst'), may hold values from -6 to 6
Outputs:
- mamba_one: bfloat16 [96, 8192], P('inst', 'tp')
- attn_one: bfloat16 [96, 8192], P('inst')
- mamba_two: bfloat16 [96, 8192], P('inst', 'tp')
- attn_two: bfloat16 [96, 8192], P('inst')
- state_out: float32 [96, 128, 64, 256], P('inst', 'tp')
Inputs may be any that keep to these rules, and one draw needn't show every extreme that they name: `migration`: column 0 of row i is a request of instance i, between i * 3 and i * 3 + 2; the last instance gives away its last request; column 1 of row i is i XOR m, for one m between 1 and 31 common to all rows. `page_table`: every device's block of 3 x 4 entries is a permutation of its 12 pool pages. `lengths`: some request reaches the largest length.
All inputs are finite; a program needn't handle non-finite values.
Results may differ from a plain program's by a relative error of at most 0.0075.
Values may be sent and summed in bfloat16 or wider, within the bound.
No kernel may reach another device: no remote copies, remote signals or barrier semaphores. Data moves between devices by JAX's collectives and lax.ppermute only.
A program may use at most 64 MiB of HBM per device.

v0:
```python
import jax
import jax.numpy as jnp
from jax import lax
from jax.sharding import PartitionSpec as P

MH = 128
HDIM = 64
STATE = 256
HPG = 32
QDIM = 128


def combined_all(value, axis, combine):
    everything = jax.tree.map(lambda part: lax.all_gather(part, axis), value)
    leading = jax.tree.map(lambda part: part[0], everything)

    def hop(k, so_far):
        return combine(so_far, jax.tree.map(lambda part: part[k], everything))

    return lax.fori_loop(1, lax.axis_size(axis), hop, leading)


def partner(value, axis, stride):
    mask = 2**stride
    pairs = [(source, source ^ mask) for source in range(lax.axis_size(axis))]
    return lax.ppermute(value, axis, pairs)


def update_state(state, x, dt_raw, bh, rate, bias):
    dt = jax.nn.softplus(dt_raw.astype(jnp.float32) + bias)
    decay = jnp.exp(-dt * rate)
    xf = x.astype(jnp.float32).reshape(state.shape[:3])
    return (
        decay[:, :, None, None] * state + (dt[:, :, None] * xf)[:, :, :, None] * bh[:, :, None, :]
    )


def read_out(state, x, z, ch, skip):
    xf = x.astype(jnp.float32).reshape(state.shape[:3])
    y = (
        jnp.einsum("nhpk,nhk->nhp", state, ch, precision=lax.Precision.HIGHEST)
        + skip[None, :, None] * xf
    )
    return y.reshape(state.shape[0], -1) * jax.nn.silu(z.astype(jnp.float32))


def group_slice(proj, group, heads):
    width = STATE
    picked = lax.dynamic_slice_in_dim(proj, group * width, width, 1).astype(jnp.float32)
    return jnp.broadcast_to(picked[:, None, :], (proj.shape[0], heads, width))


def norm_rows(gated, gain, group):
    groups = MH // HPG
    onehot = (jnp.arange(groups) == group).astype(jnp.float32)
    partial_sq = jnp.sum(gated * gated, axis=1)
    totals = lax.psum(partial_sq[:, None] * onehot[None, :], "tp")
    msq = jnp.sum(totals * onehot[None, :], axis=1) / (HPG * HDIM)
    return (gated * lax.rsqrt(msq + 1e-05)[:, None] * gain).astype(jnp.bfloat16)


def put_row(ctx, row, pos, offset):
    local = pos - offset
    hit = jnp.arange(ctx.shape[1])[None, :] == local[:, None]
    return jnp.where(hit[:, :, None], row[:, None, :], ctx)


def combine_parts(first, second):
    top = jnp.maximum(first[0], second[0])
    left = jnp.exp(first[0] - top)
    right = jnp.exp(second[0] - top)
    return (
        top,
        first[1] * left + second[1] * right,
        first[2] * left[..., None] + second[2] * right[..., None],
    )


def attend(query, ctx, upto, offset):
    rows, span, width = ctx.shape
    kvheads = width // (2 * QDIM)
    half = width // 2
    keys = ctx[:, :, :half].astype(jnp.float32).reshape(rows, span, kvheads, QDIM)
    vals = ctx[:, :, half:].astype(jnp.float32).reshape(rows, span, kvheads, QDIM)
    qf = query.astype(jnp.float32).reshape(rows, kvheads, -1, QDIM)
    scores = jnp.einsum("rgqd,rcgd->rgqc", qf, keys, precision=lax.Precision.HIGHEST) / jnp.sqrt(
        jnp.float32(QDIM)
    )
    valid = (offset + jnp.arange(span))[None, :] <= upto[:, None]
    scores = jnp.where(valid[:, None, None, :], scores, -1e30)
    top = jnp.max(scores, axis=-1)
    weights = jnp.where(valid[:, None, None, :], jnp.exp(scores - top[..., None]), 0.0)
    total = jnp.sum(weights, axis=-1)
    acc = jnp.einsum("rgqc,rcgd->rgqd", weights, vals, precision=lax.Precision.HIGHEST)
    top, total, acc = combined_all((top, total, acc), "tp", combine_parts)
    return (acc / total[..., None]).reshape(rows, -1).astype(jnp.bfloat16)


def shards(
    x_one,
    z_one,
    dt_one,
    b_one,
    c_one,
    q_one,
    kv_one,
    state,
    cache,
    page_table,
    lengths,
    migration,
    decay_rate,
    dt_bias,
    skip_gain,
    norm_gain,
    x_two,
    z_two,
    dt_two,
    b_two,
    c_two,
    q_two,
    kv_two,
):
    tp_rank = lax.axis_index("tp")
    inst_rank = lax.axis_index("inst")
    n_inst = lax.axis_size("inst")
    req, heads = (state.shape[0], state.shape[1])
    group = tp_rank * heads // HPG
    width = cache.shape[2]
    span = page_table.shape[1] * cache.shape[1]
    offset = tp_rank * span
    own_len = lax.dynamic_slice_in_dim(lengths, inst_rank * req, req)
    local_ctx = cache[page_table.reshape(-1)].reshape(req, span, width)
    state1 = update_state(
        state, x_one, dt_one, group_slice(b_one, group, heads), decay_rate, dt_bias
    )
    mamba_one = norm_rows(
        read_out(state1, x_one, z_one, group_slice(c_one, group, heads), skip_gain),
        norm_gain,
        group,
    )
    ctx1 = put_row(local_ctx, kv_one, own_len, offset)
    attn_one = attend(q_one, ctx1, own_len, offset)
    pairing = migration[0, 1]
    source = jnp.bitwise_xor(inst_rank, pairing)
    out_slot = migration[inst_rank, 0] - inst_rank * req
    mover_len = lengths[migration[source, 0]][None]

    def row_of(array):
        return lax.dynamic_slice_in_dim(array, out_slot, 1, 0)

    moving_state = row_of(state1)
    moving_pages = row_of(ctx1).reshape(1, -1)
    n_bits = n_inst.bit_length() - 1
    bit_order = list(range(n_bits))
    for bit in bit_order:
        crossing = jnp.bitwise_and(jnp.right_shift(pairing, bit), 1) == 1
        other_state = partner(moving_state, "inst", bit)
        moving_state = jnp.where(crossing, other_state, moving_state)
        other_pages = partner(moving_pages, "inst", bit)
        moving_pages = jnp.where(crossing, other_pages, moving_pages)
    arrived_ctx = moving_pages.reshape(1, span, width)
    is_new = jnp.arange(req) == out_slot
    state_in = jnp.where(is_new[:, None, None, None], moving_state, state1)
    ctx_in = jnp.where(is_new[:, None, None], arrived_ctx, ctx1)
    len_two = jnp.where(is_new, mover_len, own_len) + 1
    state_out = update_state(
        state_in, x_two, dt_two, group_slice(b_two, group, heads), decay_rate, dt_bias
    )
    mamba_two = norm_rows(
        read_out(state_out, x_two, z_two, group_slice(c_two, group, heads), skip_gain),
        norm_gain,
        group,
    )
    ctx2 = put_row(ctx_in, kv_two, len_two, offset)
    attn_two = attend(q_two, ctx2, len_two, offset)
    return (mamba_one, attn_one, mamba_two, attn_two, state_out)


def solution(mesh):
    return jax.shard_map(
        shards,
        mesh=mesh,
        in_specs=(
            P("inst", "tp"),
            P("inst", "tp"),
            P("inst", "tp"),
            P("inst", None),
            P("inst", None),
            P("inst", None),
            P("inst", None),
            P("inst", "tp", None, None),
            P("inst", None, "tp"),
            P("inst", "tp"),
            P(),
            P(),
            P("tp"),
            P("tp"),
            P("tp"),
            P("tp"),
            P("inst", "tp"),
            P("inst", "tp"),
            P("inst", "tp"),
            P("inst", None),
            P("inst", None),
            P("inst", None),
            P("inst", None),
        ),
        out_specs=(
            P("inst", "tp"),
            P("inst", None),
            P("inst", "tp"),
            P("inst", None),
            P("inst", "tp", None, None),
        ),
        check_vma=False,
    )
```

profile of v0, /device:TPU:64, one launch (start us, length us, event | category | flops | bytes accessed | tf_op | source)
XLA Modules:
  0.0 545.4 jit_solution(1164839136816281672)
XLA Ops:
  20.9 3.5 collective-permute-start.5
  25.3 1.7 multiply_add_fusion.1
  27.9 2.3 collective-permute-start
  32.5 5.4 collective-permute-done.5
  37.9 2.7 broadcast_select_fusion
  40.6 5.1 collective-permute-start.6
  46.4 15.3 %collective-permute-done.6 = bf16[1,131072]{1,0:T(2,128)(2,1)} collective-permute-done((bf16[1,131072]{1,0:T(2,128)(2,1)}, bf16[1,131072]{1,0:T(2,128)(2,1)}, u32[]{:S(2)}, u32[]{:S(2)}) %collective-permute-start.6) | collective-permute-done | bytes 262176 | tf_op jit(solution)/shard_map/ppermute | solution.py:26
  61.7 2.7 broadcast_select_fusion.1
  64.3 3.8 collective-permute-start.7
  70.3 25.3 %collective-permute-done.7 = bf16[1,131072]{1,0:T(2,128)(2,1)} collective-permute-done((bf16[1,131072]{1,0:T(2,128)(2,1)}, bf16[1,131072]{1,0:T(2,128)(2,1)}, u32[]{:S(2)}, u32[]{:S(2)}) %collective-permute-start.7) | collective-permute-done | bytes 262176 | tf_op jit(solution)/shard_map/ppermute | solution.py:26
  95.6 1.9 broadcast_select_fusion.2
  97.5 1.9 collective-permute-start.8
  99.4 60.2 %all-gather = f32[48,8,8]{2,1,0:T(8,128)S(1)} all-gather(f32[3,8,8]{2,1,0:T(8,128)S(1)} %get-tuple-element.430), channel_id=2, replica_groups=mesh['inst'=32,'tp'=16] {'tp'}, dimensions={0}, use_global_device_ids=true | all-gather | bytes 13056 | tf_op jit(solution)/shard_map/all_gather | solution.py:14
  159.6 34.5 %all-gather.1 = f32[48,8,8]{2,1,0:T(8,128)S(1)} all-gather(f32[3,8,8]{2,1,0:T(8,128)S(1)} %fusion.21), channel_id=3, replica_groups=mesh['inst'=32,'tp'=16] {'tp'}, dimensions={0}, use_global_device_ids=true | all-gather | bytes 13056 | tf_op jit(solution)/shard_map/all_gather | solution.py:14
  194.8 1.9 collective-permute-start.1
  197.6 8.7 %collective-permute-start.9 = (bf16[1,131072]{1,0:T(2,128)(2,1)S(1)}, bf16[1,131072]{1,0:T(2,128)(2,1)S(1)}, u32[]{:S(2)}, u32[]{:S(2)}) collective-permute-start(bf16[1,131072]{1,0:T(2,128)(2,1)S(1)} %broadcast_select_fusion.3), channel_id=1, source_target_pairs={{0,256},{16,272},{32,288},{48,304},{64,320},{80,336},{96,352},{112... | collective-permute-start | bytes 786440 | tf_op jit(solution)/shard_map/ppermute | solution.py:26
  206.3 6.1 %collective-permute-done.1 = f32[1,8,64,256]{3,2,1,0:T(8,128)S(1)} collective-permute-done((f32[1,8,64,256]{3,2,1,0:T(8,128)S(1)}, f32[1,8,64,256]{3,2,1,0:T(8,128)S(1)}, u32[]{:S(2)}, u32[]{:S(2)}) %collective-permute-start.1) | collective-permute-done | bytes 524320 | tf_op jit(solution)/shard_map/ppermute | solution.py:26
  213.2 1.9 collective-permute-start.2
  215.2 1.4 fusion.37
  216.6 19.8 %collective-permute-done.9 = bf16[1,131072]{1,0:T(2,128)(2,1)S(1)} collective-permute-done((bf16[1,131072]{1,0:T(2,128)(2,1)S(1)}, bf16[1,131072]{1,0:T(2,128)(2,1)S(1)}, u32[]{:S(2)}, u32[]{:S(2)}) %collective-permute-start.9) | collective-permute-done | bytes 262176 | tf_op jit(solution)/shard_map/ppermute | solution.py:26
  236.4 2.2 fusion.10
  238.7 21.2 %collective-permute-done.2 = f32[1,8,64,256]{3,2,1,0:T(8,128)} collective-permute-done((f32[1,8,64,256]{3,2,1,0:T(8,128)}, f32[1,8,64,256]{3,2,1,0:T(8,128)}, u32[]{:S(2)}, u32[]{:S(2)}) %collective-permute-start.2) | collective-permute-done | bytes 524320 | tf_op jit(solution)/shard_map/ppermute | solution.py:26
  261.0 1.9 collective-permute-start.3
  263.3 21.5 %collective-permute-done.3 = f32[1,8,64,256]{3,2,1,0:T(8,128)S(1)} collective-permute-done((f32[1,8,64,256]{3,2,1,0:T(8,128)S(1)}, f32[1,8,64,256]{3,2,1,0:T(8,128)S(1)}, u32[]{:S(2)}, u32[]{:S(2)}) %collective-permute-start.3) | collective-permute-done | bytes 524320 | tf_op jit(solution)/shard_map/ppermute | solution.py:26
  284.9 4.6 collective-permute-start.4
  289.8 70.0 %all-gather.3 = f32[48,8,8]{2,1,0:T(8,128)S(1)} all-gather(f32[3,8,8]{2,1,0:T(8,128)S(1)} %get-tuple-element.432), channel_id=5, replica_groups=mesh['inst'=32,'tp'=16] {'tp'}, dimensions={0}, use_global_device_ids=true | all-gather | bytes 13056 | tf_op jit(solution)/shard_map/all_gather | solution.py:14
  360.0 35.8 %all-gather.4 = f32[48,8,8]{2,1,0:T(8,128)S(1)} all-gather(f32[3,8,8]{2,1,0:T(8,128)S(1)} %fusion.22), channel_id=6, replica_groups=mesh['inst'=32,'tp'=16] {'tp'}, dimensions={0}, use_global_device_ids=true | all-gather | bytes 13056 | tf_op jit(solution)/shard_map/all_gather | solution.py:14
  397.1 2.0 multiply_add_fusion
  399.2 1.4 fusion.35
  401.2 79.7 %all-reduce = (f32[3,4]{1,0:T(4,128)S(1)}, f32[3,4]{1,0:T(4,128)S(1)}) all-reduce(f32[3,4]{1,0:T(4,128)S(1)} %get-tuple-element.427, f32[3,4]{1,0:T(4,128)S(1)} %get-tuple-element.426), channel_id=1, replica_groups=mesh['inst'=32,'tp'=16] {'tp'}, use_global_device_ids=true, to_apply=%region_8.9 | all-reduce | flops 24 | bytes 192 | tf_op jit(solution)/shard_map/psum | solution.py:57
  482.6 26.9 %while.38 = (s32[]{:T(128)}, f32[3,8,8]{2,1,0:T(8,128)S(1)}, f32[3,8,8]{2,1,0:T(8,128)S(1)}, f32[3,8,8,128]{3,2,1,0:T(8,128)S(1)}, f32[16,3,8,8]{3,2,1,0:T(8,128...) while((s32[]{:T(128)}, f32[3,8,8]{2,1,0:T(8,128)S(1)}, ...), condition=%wide.region_6.7_spmd, body=%wide.region_5.6_spmd.sunk | while | flops 74885 | bytes 302735 | solution.py:20
  510.6 27.1 %while.39 = (s32[]{:T(128)}, f32[3,8,8]{2,1,0:T(8,128)S(1)}, f32[3,8,8]{2,1,0:T(8,128)S(1)}, f32[3,8,8,128]{3,2,1,0:T(8,128)S(1)}, f32[16,3,8,8]{3,2,1,0:T(8,128...) while((s32[]{:T(128)}, f32[3,8,8]{2,1,0:T(8,128)S(1)}, ...), condition=%wide.region_13.14_spmd, body=%wide.region_12.13_spmd.sunk | while | flops 74885 | bytes 302735 | solution.py:20
  (169 shorter events, 77.1 us)
Async XLA Ops:
  7.2 9.4 %copy-start = (bf16[12,16,2048]{2,1,0:T(8,128)(2,1)S(1)}, bf16[12,16,2048]{2,1,0:T(8,128)(2,1)}, u32[]{:S(2)}) copy-start(bf16[12,16,2048]{2,1,0:T(8,128)(2,1)} %param.35) | copy-start | bytes 2359300
  7.2 10.0 %copy-start.5 = (bf16[3,2048]{1,0:T(4,128)(2,1)S(1)}, bf16[3,2048]{1,0:T(4,128)(2,1)}, u32[]{:S(2)}) copy-start(bf16[3,2048]{1,0:T(4,128)(2,1)} %param.33) | copy-start | bytes 36868
  7.2 474.5 %all-gather.9.cloned.1.call-start = ((), (), s32[]{:S(2)}) async-start(), calls=%async_computation | async-start | bytes 1671168 | tf_op jit(solution)/shard_map/all_gather | solution.py:14
  17.2 0.8 copy-start.17
  17.4 7.0 %copy-start.7 = (bf16[3,512]{1,0:T(4,128)(2,1)S(1)}, bf16[3,512]{1,0:T(4,128)(2,1)}, u32[]{:S(2)}) copy-start(bf16[3,512]{1,0:T(4,128)(2,1)} %param.27) | copy-start | bytes 9220
  17.4 7.1 %copy-start.12 = (bf16[3,8]{1,0:T(4,128)(2,1)S(1)}, bf16[3,8]{1,0:T(4,128)(2,1)}, u32[]{:S(2)}) copy-start(bf16[3,8]{1,0:T(4,128)(2,1)} %param.45) | copy-start | bytes 148
  17.4 7.1 %copy-start.13 = (bf16[3,8]{1,0:T(4,128)(2,1)S(1)}, bf16[3,8]{1,0:T(4,128)(2,1)}, u32[]{:S(2)}) copy-start(bf16[3,8]{1,0:T(4,128)(2,1)} %param.29) | copy-start | bytes 148
  17.5 7.0 %copy-start.15 = (f32[8]{0:T(128)S(1)}, f32[8]{0:T(128)}, u32[]{:S(2)}) copy-start(f32[8]{0:T(128)} %param.39) | copy-start | bytes 100
  17.5 7.0 %copy-start.16 = (f32[8]{0:T(128)S(1)}, f32[8]{0:T(128)}, u32[]{:S(2)}) copy-start(f32[8]{0:T(128)} %param.40) | copy-start | bytes 100
  19.6 490.1 %all-gather.11.cloned.1.call-start = ((), (), s32[]{:S(2)}) async-start(), calls=%async_computation.1 | async-start | bytes 1671168 | tf_op jit(solution)/shard_map/all_gather | solution.py:14
  20.9 17.0 %collective-permute-start.5 = (bf16[1,131072]{1,0:T(2,128)(2,1)}, bf16[1,131072]{1,0:T(2,128)(2,1)}, u32[]{:S(2)}, u32[]{:S(2)}) collective-permute-start(bf16[1,131072]{1,0:T(2,128)(2,1)} %bitcast.40), channel_id=1, source_target_pairs={{0,16},{16,0},{32,48},{48,32},{64,80},{80,64},{96,112},{112,96},{1... | collective-permute-start | bytes 786440 | tf_op jit(solution)/shard_map/ppermute | solution.py:26
  27.9 166.9 %collective-permute-start = (f32[1,8,64,256]{3,2,1,0:T(8,128)}, f32[1,8,64,256]{3,2,1,0:T(8,128)}, u32[]{:S(2)}, u32[]{:S(2)}) collective-permute-start(f32[1,8,64,256]{3,2,1,0:T(8,128)} %constant_dynamic-slice_fusion.1), channel_id=1, source_target_pairs={{0,16},{16,0},{32,48},{48,32},{64,80},{80,64},{96,112},{112,96},{1... | collective-permute-start | bytes 1572872 | tf_op jit(solution)/shard_map/ppermute | solution.py:26
  32.5 37.7 %copy-start.8 = (bf16[3,512]{1,0:T(4,128)(2,1)S(1)}, bf16[3,512]{1,0:T(4,128)(2,1)}, u32[]{:S(2)}) copy-start(bf16[3,512]{1,0:T(4,128)(2,1)} %param.43) | copy-start | bytes 9220
  40.6 21.1 %collective-permute-start.6 = (bf16[1,131072]{1,0:T(2,128)(2,1)}, bf16[1,131072]{1,0:T(2,128)(2,1)}, u32[]{:S(2)}, u32[]{:S(2)}) collective-permute-start(bf16[1,131072]{1,0:T(2,128)(2,1)} %broadcast_select_fusion), channel_id=1, source_target_pairs={{0,32},{16,48},{32,0},{48,16},{64,96},{80,112},{96,64},{112,80},{1... | collective-permute-start | bytes 786440 | tf_op jit(solution)/shard_map/ppermute | solution.py:26
  64.3 31.3 %collective-permute-start.7 = (bf16[1,131072]{1,0:T(2,128)(2,1)}, bf16[1,131072]{1,0:T(2,128)(2,1)}, u32[]{:S(2)}, u32[]{:S(2)}) collective-permute-start(bf16[1,131072]{1,0:T(2,128)(2,1)} %broadcast_select_fusion.1), channel_id=1, source_target_pairs={{0,64},{16,80},{32,96},{48,112},{64,0},{80,16},{96,32},{112,48},{1... | collective-permute-start | bytes 786440 | tf_op jit(solution)/shard_map/ppermute | solution.py:26
  97.5 99.3 %collective-permute-start.8 = (bf16[1,131072]{1,0:T(2,128)(2,1)S(1)}, bf16[1,131072]{1,0:T(2,128)(2,1)S(1)}, u32[]{:S(2)}, u32[]{:S(2)}) collective-permute-start(bf16[1,131072]{1,0:T(2,128)(2,1)S(1)} %broadcast_select_fusion.2), channel_id=1, source_target_pairs={{0,128},{16,144},{32,160},{48,176},{64,192},{80,208},{96,224},{112... | collective-permute-start | bytes 786440 | tf_op jit(solution)/shard_map/ppermute | solution.py:26
  194.1 0.7 copy-start.2
  194.8 17.6 %collective-permute-start.1 = (f32[1,8,64,256]{3,2,1,0:T(8,128)S(1)}, f32[1,8,64,256]{3,2,1,0:T(8,128)S(1)}, u32[]{:S(2)}, u32[]{:S(2)}) collective-permute-start(f32[1,8,64,256]{3,2,1,0:T(8,128)S(1)} %broadcast_select_fusion.5), channel_id=1, source_target_pairs={{0,32},{16,48},{32,0},{48,16},{64,96},{80,112},{96,64},{112,80},{1... | collective-permute-start | bytes 1572872 | tf_op jit(solution)/shard_map/ppermute | solution.py:26
  197.6 38.8 %collective-permute-start.9 = (bf16[1,131072]{1,0:T(2,128)(2,1)S(1)}, bf16[1,131072]{1,0:T(2,128)(2,1)S(1)}, u32[]{:S(2)}, u32[]{:S(2)}) collective-permute-start(bf16[1,131072]{1,0:T(2,128)(2,1)S(1)} %broadcast_select_fusion.3), channel_id=1, source_target_pairs={{0,256},{16,272},{32,288},{48,304},{64,320},{80,336},{96,352},{112... | collective-permute-start | bytes 786440 | tf_op jit(solution)/shard_map/ppermute | solution.py:26
  213.2 46.6 %collective-permute-start.2 = (f32[1,8,64,256]{3,2,1,0:T(8,128)}, f32[1,8,64,256]{3,2,1,0:T(8,128)}, u32[]{:S(2)}, u32[]{:S(2)}) collective-permute-start(f32[1,8,64,256]{3,2,1,0:T(8,128)} %broadcast_select_fusion.6), channel_id=1, source_target_pairs={{0,64},{16,80},{32,96},{48,112},{64,0},{80,16},{96,32},{112,48},{1... | collective-permute-start | bytes 1572872 | tf_op jit(solution)/shard_map/ppermute | solution.py:26
  216.6 46.3 %copy-start.6 = (bf16[3,2048]{1,0:T(4,128)(2,1)S(1)}, bf16[3,2048]{1,0:T(4,128)(2,1)}, u32[]{:S(2)}) copy-start(bf16[3,2048]{1,0:T(4,128)(2,1)} %param.49) | copy-start | bytes 36868
  261.0 23.8 %collective-permute-start.3 = (f32[1,8,64,256]{3,2,1,0:T(8,128)S(1)}, f32[1,8,64,256]{3,2,1,0:T(8,128)S(1)}, u32[]{:S(2)}, u32[]{:S(2)}) collective-permute-start(f32[1,8,64,256]{3,2,1,0:T(8,128)S(1)} %broadcast_select_fusion.7), channel_id=1, source_target_pairs={{0,128},{16,144},{32,160},{48,176},{64,192},{80,208},{96,224},{112... | collective-permute-start | bytes 1572872 | tf_op jit(solution)/shard_map/ppermute | solution.py:26
  263.2 26.2 %copy-start.18 = (bf16[3,8192]{1,0:T(4,128)(2,1)S(1)}, bf16[3,8192]{1,0:T(4,128)(2,1)}, u32[]{:S(2)}) copy-start(bf16[3,8192]{1,0:T(4,128)(2,1)} %param.48) | copy-start | bytes 147460
  284.9 112.2 %collective-permute-start.4 = (f32[1,8,64,256]{3,2,1,0:T(8,128)S(1)}, f32[1,8,64,256]{3,2,1,0:T(8,128)S(1)}, u32[]{:S(2)}, u32[]{:S(2)}) collective-permute-start(f32[1,8,64,256]{3,2,1,0:T(8,128)S(1)} %broadcast_select_fusion.8), channel_id=1, source_target_pairs={{0,256},{16,272},{32,288},{48,304},{64,320},{80,336},{96,352},{112... | collective-permute-start | bytes 1572872 | tf_op jit(solution)/shard_map/ppermute | solution.py:26
  359.8 37.3 %copy-start.3 = (f32[48,8,8]{2,1,0:T(8,128)}, f32[48,8,8]{2,1,0:T(8,128)S(1)}, u32[]{:S(2)}) copy-start(f32[48,8,8]{2,1,0:T(8,128)S(1)} %all-gather.3) | copy-start | bytes 36868
  395.9 1.3 copy-start.4
  399.1 83.5 %copy-start.1 = (f32[3,8,64,256]{3,2,1,0:T(8,128)}, f32[3,8,64,256]{3,2,1,0:T(8,128)S(1)}, u32[]{:S(2)}) copy-start(f32[3,8,64,256]{3,2,1,0:T(8,128)S(1)} %multiply_add_fusion) | copy-start | bytes 4718596
  399.1 1.5 copy-start.14
  399.2 1.7 copy-start.9
  399.2 1.8 copy-start.10
  399.2 81.9 %copy-start.11 = (f32[512]{0:T(512)S(1)}, f32[512]{0:T(512)}, u32[]{:S(2)}) copy-start(f32[512]{0:T(512)} %param.42) | copy-start | bytes 6148
Sparse Core Ops, SparseCore 0:
  19.7 88.8 all-gather.8
  397.1 77.7 all-gather.10
where the time goes:
time: 550 us; the launch traced here: 545 us
  blocking collectives  280 us (51%)
  waiting for transfers between devices  115 us (21%)
  other arithmetic  75.4 us (14%)
  starting transfers between devices  35.7 us (6%)
  between operations  21.1 us (4%)
  local copies, waits for them, and re-layouts  11.6 us (2%)
  matrix products  5.91 us (1%)
    all_gather x4, blocking collectives, combined_all(): everything = jax.tree.map(lambda part: lax.all_gather(part, axis), value)  200 us
    ppermute x10, waiting for transfers between devices, partner(): return lax.ppermute(value, axis, pairs)  115 us
    psum x1, blocking collectives, norm_rows(): totals = lax.psum(partial_sq[:, None] * onehot[None, :], 'tp')  79.7 us
    ppermute x10, starting transfers between devices, partner(): return lax.ppermute(value, axis, pairs)  35.7 us
    add x30, other arithmetic, combine_parts(): first[2] * left[..., None] + second[2] * right[..., None]  31.1 us
    add x30, other arithmetic, combine_parts(): first[1] * left + second[1] * right  22.1 us
  transfers between devices with their start and end apart: 12, of which 7 were waited for; matrix products, arithmetic and copies ran while one was open for 10% of the time, Pallas kernels for 0%

commit v1 on v0

v1 whole, which is shorter than its diff:
```python
import functools

import jax
import jax.numpy as jnp
from jax import lax
from jax.experimental import pallas as pl
from jax.experimental.pallas import tpu as pltpu
from jax.sharding import PartitionSpec as P

F32 = jnp.float32
BF16 = jnp.bfloat16

HPG = 32
QDIM = 128
STATE = 256
REQ = 3
HEADS = 8
HDIM = 64
COLS = HEADS * HDIM
KVHEADS = 8
QPK = 8
PAGE = 16
POOL = 12
PP = 4
KEYS = POOL * PAGE
EXTRA = 16
NORM = HPG * HDIM
NEG = -1e30

QH, KH = 4096, 1024
AUX = QH + KH
WIDE = AUX + 1536

VMEM = pltpu.VMEM
SMEM = pltpu.SMEM


def iota(shape, dim):
    return lax.broadcasted_iota(jnp.int32, shape, dim)


def split3(v):
    a = v.astype(BF16).astype(F32)
    rest = v - a
    b = rest.astype(BF16).astype(F32)
    c = (rest - b).astype(BF16).astype(F32)
    return a, b, c


def slot_of(mig):
    inst = lax.axis_index("inst")
    return mig[inst, 0] - inst * REQ


def call(body, out_shape, in_specs, out_specs, scratch=(), **kw):
    return pl.pallas_call(
        body,
        out_shape=out_shape,
        in_specs=in_specs,
        out_specs=out_specs,
        scratch_shapes=list(scratch),
        compiler_params=pltpu.CompilerParams(vmem_limit_bytes=40 * 2**20),
        **kw,
    )


def vm(n):
    return [pl.BlockSpec(memory_space=VMEM)] * n


def sm(n):
    return [pl.BlockSpec(memory_space=SMEM)] * n


def expand(per_head, rows):
    head = iota((rows, COLS), 1) // HDIM
    out = jnp.zeros((rows, COLS), F32)
    for h in range(HEADS):
        out = jnp.where(head == h, per_head[:, h : h + 1], out)
    return out


def softplus(v):
    return jnp.maximum(v, 0.0) + jnp.log1p(jnp.exp(-jnp.abs(v)))


def group_cols():
    g = lax.axis_index("tp") * HEADS // HPG
    return pl.ds(pl.multiple_of(g * STATE, STATE), STATE)


def prepare_body(mig, x1, dt1, b1, q2, kv2, x2, z2, dt2, b2, c2, state, out, moving, rows, held, sem):
    slot = slot_of(mig)
    copy = pltpu.make_async_copy(state.at[slot], held, sem)
    copy.start()

    def pick(v):
        v = v.astype(F32)
        return jnp.sum(jnp.where(iota(v.shape, 0) == slot, v, 0.0), axis=0, keepdims=True)

    cols = group_cols()
    rows[...] = jnp.zeros_like(rows)
    q = pick(q2[...])
    kv = pick(kv2[...])
    for k in range(2):
        rows[k : k + 1, :QH] = q[:, k * QH : (k + 1) * QH]
        rows[k : k + 1, QH:AUX] = kv[:, k * KH : (k + 1) * KH]
    rows[0:1, AUX : AUX + 512] = pick(x2[...])
    rows[0:1, AUX + 512 : AUX + 1024] = pick(z2[...])
    rows[0:1, AUX + 1024 : AUX + 1280] = pick(b2[:, cols])
    rows[0:1, AUX + 1280 : AUX + 1536] = pick(c2[:, cols])
    rows[1:2, AUX : AUX + 512] = pick(x1[...])
    rows[1:2, AUX + 512 : AUX + 768] = pick(b1[:, cols])
    rows[1:2, AUX + 768 : AUX + 776] = pick(dt2[...])
    rows[1:2, AUX + 896 : AUX + 904] = pick(dt1[...])
    out[...] = rows[...].astype(BF16)
    copy.wait()
    moving[...] = held[...].astype(BF16)


def prepare(mig, x1, dt1, b1, q2, kv2, x2, z2, dt2, b2, c2, state):
    return call(
        prepare_body,
        (
            jax.ShapeDtypeStruct((2, WIDE), BF16),
            jax.ShapeDtypeStruct(state.shape[1:], BF16),
        ),
        sm(1) + vm(10) + [pl.BlockSpec(memory_space=pl.ANY)],
        tuple(vm(2)),
        [VMEM((2, WIDE), F32), VMEM(state.shape[1:], F32), pltpu.SemaphoreType.DMA],
        name="prepare",
    )(mig, x1, dt1, b1, q2, kv2, x2, z2, dt2, b2, c2, state)


def stats_row(col, sub, lane):
    a, b, c = split3(jnp.broadcast_to(col, col.shape[:2] + (128,)))
    row = jnp.where(
        lane == sub,
        a,
        jnp.where(lane == sub + 8, b, jnp.where(lane == sub + 16, c, 0.0)),
    )
    return jnp.sum(row, axis=1, keepdims=True)


def stats_col(row, sub, lane):
    spread = jnp.broadcast_to(row, (row.shape[0], 8, 128))
    mine = jnp.logical_and(lane < 24, lane % 8 == sub)
    return jnp.sum(jnp.where(mine, spread, 0.0), axis=2, keepdims=True)


def partial_body(
    mig, lens, table, swapped, x1, z1, dt1, b1, c1, q1, kv1, state, cache,
    rate, bias, skip, x2, z2, dt2, b2, c2, q2, kv2,
    blocks, gated, q8, kv16, x8, z8, d8, b8, c8,
):
    slot = slot_of(mig)
    inst = lax.axis_index("inst")
    tp = lax.axis_index("tp")
    cols = group_cols()
    sw = swapped[...].astype(F32)

    def rows8(scr, one, two, moved):
        n = one.shape[-1]
        scr[...] = jnp.zeros_like(scr)
        scr[0:3, :n] = one.astype(F32)
        scr[3:6, :n] = jnp.where(iota((3, n), 0) == slot, moved, two.astype(F32))
        return scr[...]

    q8[6:8, :] = jnp.zeros_like(q8[6:8, :])
    q8[0:3, :] = q1[...].astype(F32)
    q8[3:6, :] = q2[...].astype(F32)
    for k in range(2):
        here = pl.ds(k * QH, QH)
        q8[3:6, here] = jnp.where(iota((3, QH), 0) == slot, sw[k : k + 1, :QH], q8[3:6, here])
    kv16[...] = jnp.zeros_like(kv16)
    kv16[0:3, :] = kv1[...].astype(F32)
    for k in range(2):
        here = pl.ds(k * KH, KH)
        kv16[3:6, here] = jnp.where(
            iota((3, KH), 0) == slot, sw[k : k + 1, QH:AUX], kv2[:, here].astype(F32)
        )

    xx = rows8(x8, x1[...], x2[...], sw[0:1, AUX : AUX + 512])
    zz = rows8(z8, z1[...], z2[...], sw[0:1, AUX + 512 : AUX + 1024])
    bb = rows8(b8, b1[:, cols], b2[:, cols], sw[0:1, AUX + 1024 : AUX + 1280])
    cc = rows8(c8, c1[:, cols], c2[:, cols], sw[0:1, AUX + 1280 : AUX + 1536])
    dd = rows8(d8, dt1[...], dt2[...], sw[1:2, AUX + 768 : AUX + 776])
    dt = softplus(expand(dd, 8) + expand(bias[...], 1))
    decay = jnp.exp(-dt * expand(rate[...], 1))
    read = jnp.zeros((8, COLS), F32)
    row256 = iota((8, STATE), 0)
    for r in range(REQ):
        ch = jnp.where(jnp.logical_or(row256 == r, row256 == r + 3), cc, 0.0).astype(BF16)
        s = state[r].reshape(COLS, STATE)
        hi = s.astype(BF16)
        lo = (s - hi.astype(F32)).astype(BF16)
        for part in (hi, lo):
            read += lax.dot_general(ch, part, (((1,), (1,)), ((), ())), preferred_element_type=F32)
    pushed = dt * xx
    same = jnp.sum(bb * cc, axis=1, keepdims=True)
    cross = jnp.sum(pltpu.roll(bb, 3, 0) * cc, axis=1, keepdims=True)
    first = pltpu.roll(decay, 3, 0) * read + pltpu.roll(pushed, 3, 0) * cross
    second = iota((8, COLS), 0) >= 3
    y = decay * jnp.where(second, first, read) + pushed * same + expand(skip[...], 1) * xx
    g = y * (zz / (1.0 + jnp.exp(-zz)))
    gated[...] = g
    squares = jnp.sum(g * g, axis=1, keepdims=True)

    lane = iota((1, KEYS + EXTRA), 1)
    owner = jnp.full(lane.shape, -1, jnp.int32)
    ok = jnp.zeros(lane.shape, jnp.int32)
    late = jnp.logical_and(lane >= KEYS + REQ, lane < KEYS + 2 * REQ)
    span = PP * PAGE
    for r in range(REQ):
        length = lens[inst * REQ + r]
        for p in range(PP):
            here = (lane // PAGE) == table[r, p]
            pos = tp * span + p * PAGE + lane % PAGE
            owner = jnp.where(here, r, owner)
            ok = jnp.where(jnp.logical_and(here, pos < length), 1, ok)
        for e, at in ((r, length), (r + REQ, length + 1)):
            here = lane == KEYS + e
            owner = jnp.where(here, r, owner)
            ok = jnp.where(jnp.logical_and(here, at // span == tp), 1, ok)
    row = iota((8, KEYS + EXTRA), 0)
    mine = jnp.where(row < 3, row, jnp.where(row < 6, row - 3, -2))
    valid = (mine == owner) & (ok == 1) & ((row >= 3) | jnp.logical_not(late))
    valid = valid.astype(F32)[None]
    sub = iota((QPK, 8, 128), 1)
    lane3 = iota((QPK, 8, 128), 2)
    sq_row = stats_row(jnp.broadcast_to(squares[None], (1, 8, 1)), sub[:1], lane3[:1])
    extra = kv16[...].astype(BF16)
    for k in range(KVHEADS):
        qk = jnp.concatenate(
            [q8[:, (k * QPK + h) * QDIM : (k * QPK + h + 1) * QDIM] for h in range(QPK)], axis=0
        ).astype(BF16)
        kcols = slice(k * QDIM, (k + 1) * QDIM)
        vcols = slice((KVHEADS + k) * QDIM, (KVHEADS + k + 1) * QDIM)
        keys = jnp.concatenate([cache[:, :, kcols].reshape(KEYS, QDIM), extra[:, kcols]], axis=0)
        vals = jnp.concatenate([cache[:, :, vcols].reshape(KEYS, QDIM), extra[:, vcols]], axis=0)
        s = lax.dot_general(qk, keys, (((1,), (1,)), ((), ())), preferred_element_type=F32)
        s = (s * (1.0 / QDIM**0.5)).reshape(QPK, 8, KEYS + EXTRA)
        s = jnp.where(valid > 0.0, s, NEG)
        top = jnp.max(s, axis=2, keepdims=True)
        w = jnp.where(valid > 0.0, jnp.exp(s - top), 0.0).astype(BF16)
        total = jnp.sum(w.astype(F32), axis=2, keepdims=True)
        acc = jnp.dot(
            w.reshape(QPK * 8, KEYS + EXTRA), vals, preferred_element_type=F32
        ).reshape(QPK, 8, QDIM)
        some = total > 0.0
        safe = jnp.where(some, total, 1.0)
        lse = jnp.where(some, top + jnp.log(safe), NEG)
        o = acc / safe
        o = jnp.where(sub == 6, stats_row(lse, sub, lane3), jnp.where(sub == 7, sq_row, o))
        blocks[k] = o.reshape(QPK * 8, QDIM).astype(BF16)


def partials(mig, lens, table, swapped, *rest):
    return call(
        partial_body,
        (
            jax.ShapeDtypeStruct((KVHEADS, QPK * 8, QDIM), BF16),
            jax.ShapeDtypeStruct((8, COLS), F32),
        ),
        sm(3) + vm(1 + len(rest)),
        tuple(vm(2)),
        [
            VMEM((8, KVHEADS * QPK * QDIM), F32),
            VMEM((EXTRA, 2 * KVHEADS * QDIM), F32),
            VMEM((8, COLS), F32),
            VMEM((8, COLS), F32),
            VMEM((8, 128), F32),
            VMEM((8, STATE), F32),
            VMEM((8, STATE), F32),
        ],
        name="partials",
    )(mig, lens, table, swapped, *rest)


def combine_body(mig, recv, gated, mine, moved, scr):
    slot = slot_of(mig)
    x = lax.axis_index("tp") // 4
    sub = iota((QPK, 8, 128), 1)
    lane = iota((QPK, 8, 128), 2)
    lses = []
    for j in range(8):
        rows = recv[j].astype(F32).reshape(QPK, 8, 128)
        lses.append(stats_col(rows[:, 6:7, :], sub, lane))
    top = functools.reduce(jnp.maximum, lses)
    total = jnp.zeros_like(top)
    acc = jnp.zeros((QPK, 8, 128), F32)
    for j in range(8):
        w = jnp.exp(lses[j] - top)
        total += w
        acc += w * recv[j].astype(F32).reshape(QPK, 8, 128)
    o = acc / total
    lse = top + jnp.log(total)
    pair = recv[2 * x].astype(F32)[7:8] + recv[2 * x + 1].astype(F32)[7:8]
    squares = stats_col(pair[None], sub[:1], lane[:1])
    sq_row = stats_row(squares, sub[:1], lane[:1])
    block = jnp.where(sub == 6, stats_row(lse, sub, lane), jnp.where(sub == 7, sq_row, o))
    mine[...] = block.reshape(QPK * 8, 128).astype(BF16)

    here = sub == slot + 3
    lane2 = iota((QPK, 128), 1)

    def terms(v):
        a, b, c = split3(v)
        return jnp.where(lane2 == 0, a, jnp.where(lane2 == 1, b, jnp.where(lane2 == 2, c, 0.0)))

    scr[0:8, :] = jnp.sum(jnp.where(here, o, 0.0), axis=1)
    scr[8:16, :] = terms(jnp.sum(jnp.where(here, lse, 0.0), axis=1))
    g = gated[...]
    g = jnp.sum(jnp.where(iota(g.shape, 0) == slot + 3, g, 0.0), axis=0, keepdims=True)
    hi = g.astype(BF16).astype(F32)
    for k in range(4):
        piece = slice(k * 128, (k + 1) * 128)
        scr[16 + k : 17 + k, :] = hi[:, piece]
        scr[20 + k : 21 + k, :] = (g - hi)[:, piece]
    sq = jnp.sum(jnp.where(here[:1], squares, 0.0), axis=1)
    scr[24:32, :] = terms(jnp.broadcast_to(sq, (8, 128)))
    moved[...] = scr[...].astype(BF16)


def combine(mig, recv, gated):
    return call(
        combine_body,
        (jax.ShapeDtypeStruct((QPK * 8, 128), BF16), jax.ShapeDtypeStruct((32, 128), BF16)),
        sm(1) + vm(2),
        tuple(vm(2)),
        [VMEM((32, 128), F32)],
        name="combine",
    )(mig, recv, gated)


def finish_body(mig, mine, across, near, far, gated, gain, blocks, m1, m2, scr):
    slot = slot_of(mig)
    upper = (lax.axis_index("tp") // 2) % 2 == 1
    sub = iota((QPK, 8, 128), 1)
    lane = iota((QPK, 8, 128), 2)
    own = mine[...].astype(F32).reshape(QPK, 8, 128)
    other = across[...].astype(F32).reshape(QPK, 8, 128)
    same = near[...].astype(F32)
    flip = far[...].astype(F32)

    def merge(a, b, la, lb):
        top = jnp.maximum(la, lb)
        wa = jnp.exp(la - top)
        wb = jnp.exp(lb - top)
        return (wa * a + wb * b) / (wa + wb)

    a = jnp.where(upper, other, own)
    b = jnp.where(upper, own, other)
    o = merge(a, b, stats_col(a[:, 6:7], sub, lane), stats_col(b[:, 6:7], sub, lane))
    sq = stats_col(own[:1, 7:8], sub[:1], lane[:1]) + stats_col(other[:1, 7:8], sub[:1], lane[:1])

    a = jnp.where(upper, flip, same)
    b = jnp.where(upper, same, flip)
    la = jnp.sum(a[8:16], axis=1, keepdims=True)
    lb = jnp.sum(b[8:16], axis=1, keepdims=True)
    om = merge(a[0:8], b[0:8], la, lb)
    o = jnp.where(sub == slot + 3, om[:, None, :], o)
    o = o.reshape(QPK * 8, 128).astype(BF16)
    for k in range(8):
        blocks[k] = o

    sqm = jnp.sum(same[24:25] + flip[24:25], axis=1, keepdims=True)
    gm = same[16:20] + same[20:24]
    scr[...] = gated[...]
    row = iota((8, COLS), 0) == slot + 3
    g = jnp.where(row, jnp.concatenate([gm[k : k + 1] for k in range(4)], axis=1), scr[...])
    total = jnp.where(row, sqm, sq[0])
    scr[...] = g * lax.rsqrt(total * (1.0 / NORM) + 1e-05) * gain[...]
    m1[...] = scr[0:3, :].astype(BF16)
    m2[...] = scr[3:6, :].astype(BF16)


def finish(mig, mine, across, near, far, gated, gain):
    return call(
        finish_body,
        (
            jax.ShapeDtypeStruct((8, QPK * 8, 128), BF16),
            jax.ShapeDtypeStruct((REQ, COLS), BF16),
            jax.ShapeDtypeStruct((REQ, COLS), BF16),
        ),
        sm(1) + vm(6),
        tuple(vm(3)),
        [VMEM((8, COLS), F32)],
        name="finish",
    )(mig, mine, across, near, far, gated, gain)


def spread_body(recv, a1, a2, scr):
    for k in range(KVHEADS):
        rows = recv[k].astype(F32)
        for h in range(QPK):
            at = (k * QPK + h) * QDIM
            scr[:, at : at + QDIM] = rows[h * 8 : (h + 1) * 8]
    a1[...] = scr[0:3, :].astype(BF16)
    a2[...] = scr[3:6, :].astype(BF16)


def spread(recv):
    n = KVHEADS * QPK * QDIM
    return call(
        spread_body,
        (jax.ShapeDtypeStruct((REQ, n), BF16),) * 2,
        vm(1),
        tuple(vm(2)),
        [VMEM((8, n), F32)],
        name="spread",
    )(recv)


def update_body(mig, swapped, arrived, x1, dt1, b1, rate, bias, x2, dt2, b2, state, out, x8, d8, b8):
    slot = slot_of(mig)
    r = pl.program_id(0)
    cols = group_cols()
    sw = swapped[...].astype(F32)

    def rows8(scr, one, two, moved):
        n = one.shape[-1]
        scr[...] = jnp.zeros_like(scr)
        scr[0:3, :n] = jnp.where(iota((3, n), 0) == slot, moved, one.astype(F32))
        scr[3:6, :n] = two.astype(F32)
        return scr[...]

    xx = rows8(x8, x1[...], x2[...], sw[1:2, AUX : AUX + 512])
    bb = rows8(b8, b1[:, cols], b2[:, cols], sw[1:2, AUX + 512 : AUX + 768])
    dd = rows8(d8, dt1[...], dt2[...], sw[1:2, AUX + 896 : AUX + 904])
    dt = softplus(expand(dd, 8) + expand(bias[...], 1))
    decay = jnp.exp(-dt * expand(rate[...], 1))
    pushed = dt * xx
    later = pltpu.roll(decay, 5, 0)
    row = iota((8, COLS), 0)
    u = jnp.where(row < 3, pushed * later, pushed)
    both = jnp.sum(jnp.where(row == r, decay * later, 0.0), axis=0, keepdims=True)
    mine = jnp.logical_or(row == r, row == r + 3)
    u = jnp.where(mine, u, 0.0)
    hi = u.astype(BF16)
    lo = (u - hi.astype(F32)).astype(BF16)
    bh = bb.astype(BF16)
    add = jnp.zeros((COLS, STATE), F32)
    for part in (hi, lo):
        add += lax.dot_general(part, bh, (((0,), (0,)), ((), ())), preferred_element_type=F32)
    moved = r == slot
    for h in range(HEADS):
        s = jnp.where(moved, arrived[h].astype(F32), state[0, h])
        d = both[:, h * HDIM : h * HDIM + 1]
        out[0, h] = d * s + add[h * HDIM : (h + 1) * HDIM]


def update(mig, swapped, arrived, x1, dt1, b1, rate, bias, x2, dt2, b2, state):
    block = pl.BlockSpec((1,) + state.shape[1:], lambda r: (r, 0, 0, 0))
    return call(
        update_body,
        jax.ShapeDtypeStruct(state.shape, F32),
        sm(1) + vm(10) + [block],
        block,
        [VMEM((8, COLS), F32), VMEM((8, 128), F32), VMEM((8, STATE), F32)],
        grid=(REQ,),
        name="update",
    )(mig, swapped, arrived, x1, dt1, b1, rate, bias, x2, dt2, b2, state)


PLANE = [[x * 4 + z * 2 + c for x in range(4) for c in range(2)] for z in range(2)]


def plane_exchange(blocks):
    return lax.all_to_all(blocks, "tp", 0, 0, axis_index_groups=PLANE)


def swap_by(m, flip):
    n_tp = lax.axis_size("tp")
    n = lax.axis_size("inst") * n_tp
    return [(s, s ^ (m * n_tp + flip)) for s in range(n)]


def swap_inputs(m, payload):
    return lax.ppermute(payload, ("inst", "tp"), swap_by(m, 0))


def swap_results(m, moving, mine, moved):
    arrived = lax.ppermute(moving, ("inst", "tp"), swap_by(m, 0))
    across = lax.ppermute(mine, ("inst", "tp"), swap_by(0, 2))
    far = lax.ppermute(moved, ("inst", "tp"), swap_by(m, 2))
    near = lax.ppermute(moved, ("inst", "tp"), swap_by(m, 0))
    return arrived, across, near, far


def shards(
    x_one, z_one, dt_one, b_one, c_one, q_one, kv_one, state, cache, page_table,
    lengths, migration, decay_rate, dt_bias, skip_gain, norm_gain,
    x_two, z_two, dt_two, b_two, c_two, q_two, kv_two,
):
    n_inst = lax.axis_size("inst")
    rate = decay_rate[None]
    bias = dt_bias[None]
    which = migration[0, 1] - 1
    ways = range(1, n_inst)
    payload, moving = prepare(
        migration, x_one, dt_one, b_one, q_two, kv_two, x_two, z_two, dt_two, b_two, c_two, state
    )
    swapped = lax.switch(which, [functools.partial(swap_inputs, m) for m in ways], payload)
    blocks, gated = partials(
        migration, lengths, page_table, swapped,
        x_one, z_one, dt_one, b_one, c_one, q_one, kv_one, state, cache,
        rate, bias, skip_gain[None], x_two, z_two, dt_two, b_two, c_two, q_two, kv_two,
    )
    mine, moved = combine(migration, plane_exchange(blocks), gated)
    arrived, across, near, far = lax.switch(
        which, [functools.partial(swap_results, m) for m in ways], moving, mine, moved
    )
    blocks, mamba_one, mamba_two = finish(
        migration, mine, across, near, far, gated, norm_gain[None]
    )
    attn_one, attn_two = spread(plane_exchange(blocks))
    state_out = update(
        migration, swapped, arrived, x_one, dt_one, b_one, rate, bias, x_two, dt_two, b_two, state
    )
    return (mamba_one, attn_one, mamba_two, attn_two, state_out)


def solution(mesh):
    row = P("inst", "tp")
    wide = P("inst", None)
    head = P("tp")
    states = P("inst", "tp", None, None)
    return jax.shard_map(
        shards,
        mesh=mesh,
        in_specs=(
            row, row, row, wide, wide, wide, wide, states, P("inst", None, "tp"), row,
            P(), P(), head, head, head, head, row, row, row, wide, wide, wide, wide,
        ),
        out_specs=(row, wide, row, wide, states),
        check_vma=False,
    )
```

time: 550 us -> 117 us (0.21)
  the two profiles are of different devices: /device:TPU:64 before, /device:TPU:1 now
where the time goes in v1:
time: 117 us; the launch traced here: 116 us
  starting transfers between devices  66.1 us (56%)
  waiting for transfers between devices  12.3 us (11%)
  blocking collectives  12.3 us (11%)
  local copies, waits for them, and re-layouts  11.7 us (10%)
  Pallas kernels  11.6 us (10%)
  between operations  1.61 us (1%)
    ppermute x1, starting transfers between devices, swap_results(): far = lax.ppermute(moved, ('inst', 'tp'), swap_by(m, 2))  19 us
    ppermute x1, starting transfers between devices, swap_inputs(): return lax.ppermute(payload, ('inst', 'tp'), swap_by(m, 0))  13.4 us
    all_to_all x1, blocking collectives, plane_exchange(): return lax.all_to_all(blocks, 'tp', 0, 0, axis_index_groups=PLANE)  12.3 us
    ppermute x1, starting transfers between devices, swap_results(): near = lax.ppermute(moved, ('inst', 'tp'), swap_by(m, 0))  10.5 us
    unnamed x67, local copies, waits for them, and re-layouts  10.5 us
    ppermute x1, waiting for transfers between devices, swap_results(): far = lax.ppermute(moved, ('inst', 'tp'), swap_by(m, 2))  9.19 us
    ppermute x1, starting transfers between devices, swap_results(): arrived = lax.ppermute(moving, ('inst', 'tp'), swap_by(m, 0))  8.88 us
    ppermute x1, starting transfers between devices, swap_results(): across = lax.ppermute(mine, ('inst', 'tp'), swap_by(0, 2))  8.84 us
  transfers between devices with their start and end apart: 6, of which 3 were waited for; matrix products, arithmetic and copies ran while one was open for 0% of the time, Pallas kernels for 3%

profile of v1, /device:TPU:1, one launch (start us, length us, event | category | flops | bytes accessed | tf_op | source)
XLA Modules:
  0.0 115.7 jit_solution(1448461921266900679)
XLA Ops:
  0.7 0.8 copy.31.mig
  1.5 1.2 %slice.3 = s32[1,1]{0,1:T(1,128)} slice(s32[32,2]{0,1:T(2,128)} %param.96), slice={[0:1], [1:2]} | slice | bytes 8 | tf_op jit(solution)/shard_map/slice | solution.py:499
  3.3 1.4 %copy-done = f32[3,8,64,256]{3,2,1,0:T(8,128)S(1)} copy-done((f32[3,8,64,256]{3,2,1,0:T(8,128)S(1)}, f32[3,8,64,256]{3,2,1,0:T(8,128)}, u32[]{:S(2)}) %copy-start) | copy-done | bytes 1572888
  4.7 0.8 copy-done.3
  5.6 0.7 copy-done.5
  6.3 0.7 copy-done.7
  7.0 0.7 copy-done.10
  7.7 0.7 copy-done.12
  8.4 0.7 copy-done.14
  9.1 0.7 copy-done.16
  9.8 0.7 copy-done.19
  10.5 0.7 copy-done.21
  11.1 0.7 copy-done.23
  11.9 1.1 prepare.1
  13.0 14.7 %conditional.2 = (bf16[2,6656]{1,0:T(2,128)(2,1)}) conditional(s32[]{:T(128)} %bitcast, bf16[2,6656]{1,0:T(2,128)(2,1)S(1)} %get-tuple-element.362, bf16[2,6656]{1,0:T(2,128)(2,1)S(1)} %get-tuple-element.362, bf16[2,6656]{1,0:T(2,128)(2,1)S(1)} %get-tuple-element.362, ...), branch_computations={%region_0.0_spmd, %region_1.0_spmd, %region_2.0_spmd, %region_3.0_... | conditional | bytes 106544 | solution.py:504
  13.0 13.4 %collective-permute-start.24 = (bf16[2,6656]{1,0:T(2,128)(2,1)S(1)}, bf16[2,6656]{1,0:T(2,128)(2,1)}, u32[]{:S(2)}, u32[]{:S(2)}) collective-permute-start(bf16[2,6656]{1,0:T(2,128)(2,1)S(1)} %param.24), channel_id=1, source_target_pairs={{0,400},{1,401},{2,402},{3,403},{4,404},{5,405},{6,406},{7,407},{8... | collective-permute-start | bytes 79880 | tf_op jit(solution)/shard_map/cond/branch_24_fun/ppermute | solution.py:480
  26.4 1.3 %collective-permute-done.24 = bf16[2,6656]{1,0:T(2,128)(2,1)} collective-permute-done((bf16[2,6656]{1,0:T(2,128)(2,1)S(1)}, bf16[2,6656]{1,0:T(2,128)(2,1)}, u32[]{:S(2)}, u32[]{:S(2)}) %collective-permute-start.24) | collective-permute-done | bytes 26656 | tf_op jit(solution)/shard_map/cond/branch_24_fun/ppermute | solution.py:480
  27.9 1.1 copy-done.2
  29.1 3.6 %partials.1 = (bf16[8,64,128]{2,1,0:T(8,128)(2,1)S(1)}, f32[8,512]{1,0:T(8,128)S(1)}) custom-call(s32[32,2]{1,0:T(8,128)S(1)} %copy.31.mig, s32[96]{0:T(128)S(1)} %copy-done.31, s32[3,4]{1,0:T(4,128)S(1)} %copy-done.27, bf16[2,6656]{1,0:T(2,128)(2,1)} %get-tuple-element.501.swapped, bf16[3,512]{1,0:T(4,128)(2,1)S(1)} %copy-done.13, ...), custom_call_target="tpu_custom_call" | custom-call | tf_op jit(solution)/shard_map/partials/pallas_call | solution.py:259
  32.7 12.3 %all_to_all.10.recv = bf16[8,64,128]{2,1,0:T(8,128)(2,1)S(1)} all-to-all(bf16[8,64,128]{2,1,0:T(8,128)(2,1)S(1)} %get-tuple-element.363), channel_id=1, replica_groups={{0,1,4,5,8,9,12,13},{2,3,6,7,10,11,14,15},{16,17,20,21,24,25,28,29},{18..., dimensions={0} | all-to-all | bytes 262144 | tf_op jit(solution)/shard_map/all_to_all | solution.py:470
  45.0 1.1 combine.1
  46.1 56.5 %conditional.3 = (bf16[8,64,256]{2,1,0:T(8,128)(2,1)}, bf16[64,128]{1,0:T(8,128)(2,1)}, bf16[32,128]{1,0:T(8,128)(2,1)}, bf16[32,128]{1,0:T(8,128)(2,1)}) conditional(s32[]{:T(128)} %bitcast, (bf16[8,64,256]{2,1,0:T(8,128)(2,1)S(1)}, bf16[64,128]{1,0:T(8,128)(2,1)S(1)}, bf16[32,128]{1,0:T(8,128)(2,1)S(1)}) %tuple.225, ...), branch_computations={%region_31.0_spmd, %region_32.0_spmd, %region_33.0_spmd, %region_3... | conditional | bytes 1179840 | solution.py:511
  46.1 8.9 %collective-permute-start.127 = (bf16[8,64,256]{2,1,0:T(8,128)(2,1)S(1)}, bf16[8,64,256]{2,1,0:T(8,128)(2,1)}, u32[]{:S(2)}, u32[]{:S(2)}) collective-permute-start(bf16[8,64,256]{2,1,0:T(8,128)(2,1)S(1)} %get-tuple-element.321), channel_id=1, source_target_pairs={{0,400},{1,401},{2,402},{3,403},{4,404},{5,405},{6,406},{7,407},{8... | collective-permute-start | bytes 786440 | tf_op jit(solution)/shard_map/cond/branch_24_fun/ppermute | solution.py:484
  55.0 8.8 %collective-permute-start.128 = (bf16[64,128]{1,0:T(8,128)(2,1)S(1)}, bf16[64,128]{1,0:T(8,128)(2,1)}, u32[]{:S(2)}, u32[]{:S(2)}) collective-permute-start(bf16[64,128]{1,0:T(8,128)(2,1)S(1)} %get-tuple-element.322), channel_id=1, source_target_pairs={{0,2},{1,3},{2,0},{3,1},{4,6},{5,7},{6,4},{7,5},{8,10},{9,11},{10,... | collective-permute-start | bytes 49160 | tf_op jit(solution)/shard_map/cond/branch_24_fun/ppermute | solution.py:485
  63.8 10.5 %collective-permute-start.129 = (bf16[32,128]{1,0:T(8,128)(2,1)S(1)}, bf16[32,128]{1,0:T(8,128)(2,1)}, u32[]{:S(2)}, u32[]{:S(2)}) collective-permute-start(bf16[32,128]{1,0:T(8,128)(2,1)S(1)} %get-tuple-element.323), channel_id=1, source_target_pairs={{0,400},{1,401},{2,402},{3,403},{4,404},{5,405},{6,406},{7,407},{8... | collective-permute-start | bytes 24584 | tf_op jit(solution)/shard_map/cond/branch_24_fun/ppermute | solution.py:487
  74.4 19.0 %collective-permute-start.130 = (bf16[32,128]{1,0:T(8,128)(2,1)S(1)}, bf16[32,128]{1,0:T(8,128)(2,1)}, u32[]{:S(2)}, u32[]{:S(2)}) collective-permute-start(bf16[32,128]{1,0:T(8,128)(2,1)S(1)} %get-tuple-element.323), channel_id=1, source_target_pairs={{0,402},{1,403},{2,400},{3,401},{4,406},{5,407},{6,404},{7,405},{8... | collective-permute-start | bytes 24584 | tf_op jit(solution)/shard_map/cond/branch_24_fun/ppermute | solution.py:486
  93.4 9.2 %collective-permute-done.130 = bf16[32,128]{1,0:T(8,128)(2,1)} collective-permute-done((bf16[32,128]{1,0:T(8,128)(2,1)S(1)}, bf16[32,128]{1,0:T(8,128)(2,1)}, u32[]{:S(2)}, u32[]{:S(2)}) %collective-permute-start.130) | collective-permute-done | bytes 8224 | tf_op jit(solution)/shard_map/cond/branch_24_fun/ppermute | solution.py:486
  102.6 1.6 %finish.1 = (bf16[8,64,128]{2,1,0:T(8,128)(2,1)}, bf16[3,512]{1,0:T(4,128)(2,1)}, bf16[3,512]{1,0:T(4,128)(2,1)}) custom-call(s32[32,2]{1,0:T(8,128)S(1)} %copy.31.mig, bf16[64,128]{1,0:T(8,128)(2,1)S(1)} %get-tuple-element.365.mine, bf16[64,128]{1,0:T(8,128)(2,1)} %get-tuple-element.368.across, bf16[32,128]{1,0:T(8,128)(2,1)} %get-tuple-element.369.near, ...), custom_call_target="tpu_custom_call" | custom-call | tf_op jit(solution)/shard_map/finish/pallas_call | solution.py:379
  104.2 5.5 %all-to-all-start.1 = ((bf16[8,64,128]{2,1,0:T(8,128)(2,1)}), bf16[8,64,128]{2,1,0:T(8,128)(2,1)S(1)}, u32[]{:S(2)}, u32[]{:S(2)}) async-start(bf16[8,64,128]{2,1,0:T(8,128)(2,1)} %get-tuple-element.372), calls=%async_computation.1 | async-start | bytes 262144 | tf_op jit(solution)/shard_map/all_to_all | solution.py:470
  109.7 3.5 %update.1 = f32[3,8,64,256]{3,2,1,0:T(8,128)} custom-call(s32[32,2]{1,0:T(8,128)S(1)} %copy.31.mig, bf16[2,6656]{1,0:T(2,128)(2,1)} %get-tuple-element.501.swapped, bf16[8,64,256]{2,1,0:T(8,128)(2,1)} %get-tuple-element.376.arrived, bf16[3,512]{1,0:T(4,128)(2,1)S(1)} %copy-done.13, bf16[3,8]{1,0:T(4,128)(2,1)S(1)} %copy-done.22, ...), custom_call_target="tpu_custom_call" | custom-call | tf_op jit(solution)/shard_map/update/pallas_call | solution.py:455
  113.3 1.7 %all-to-all-done.1.recv = bf16[8,64,128]{2,1,0:T(8,128)(2,1)S(1)} async-done(((bf16[8,64,128]{2,1,0:T(8,128)(2,1)}), bf16[8,64,128]{2,1,0:T(8,128)(2,1)S(1)}, u32[]{:S(2)}, u32[]{:S(2)}) %all-to-all-start.1) | async-done | bytes 131104 | tf_op jit(solution)/shard_map/all_to_all | solution.py:470
  115.0 0.7 spread.1
  (57 shorter events, 0.1 us)
Async XLA Ops:
  0.6 27.1 %copy-start.24 = (bf16[3,8]{1,0:T(4,128)(2,1)S(1)}, bf16[3,8]{1,0:T(4,128)(2,1)}, u32[]{:S(2)}) copy-start(bf16[3,8]{1,0:T(4,128)(2,1)} %dt2.5) | copy-start | bytes 148
  0.6 27.1 %copy-start.8 = (bf16[3,1024]{1,0:T(4,128)(2,1)S(1)}, bf16[3,1024]{1,0:T(4,128)(2,1)}, u32[]{:S(2)}) copy-start(bf16[3,1024]{1,0:T(4,128)(2,1)} %b2.5) | copy-start | bytes 18436
  0.7 27.1 %copy-start.13 = (bf16[3,512]{1,0:T(4,128)(2,1)S(1)}, bf16[3,512]{1,0:T(4,128)(2,1)}, u32[]{:S(2)}) copy-start(bf16[3,512]{1,0:T(4,128)(2,1)} %x1.5) | copy-start | bytes 9220
  0.7 27.1 %copy-start.22 = (bf16[3,8]{1,0:T(4,128)(2,1)S(1)}, bf16[3,8]{1,0:T(4,128)(2,1)}, u32[]{:S(2)}) copy-start(bf16[3,8]{1,0:T(4,128)(2,1)} %dt1.5) | copy-start | bytes 148
  0.7 27.1 %copy-start.6 = (bf16[3,1024]{1,0:T(4,128)(2,1)S(1)}, bf16[3,1024]{1,0:T(4,128)(2,1)}, u32[]{:S(2)}) copy-start(bf16[3,1024]{1,0:T(4,128)(2,1)} %b1.5) | copy-start | bytes 18436
  0.7 27.1 %copy-start.28 = (f32[8]{0:T(128)S(1)}, f32[8]{0:T(128)}, u32[]{:S(2)}) copy-start(f32[8]{0:T(128)} %param.97) | copy-start | bytes 100
  3.3 1.4 %copy-start = (f32[3,8,64,256]{3,2,1,0:T(8,128)S(1)}, f32[3,8,64,256]{3,2,1,0:T(8,128)}, u32[]{:S(2)}) copy-start(f32[3,8,64,256]{3,2,1,0:T(8,128)} %state.5) | copy-start | bytes 4718596
  4.7 0.8 copy-start.3
  5.6 0.7 copy-start.5
  7.0 0.7 copy-start.10
  11.8 16.0 %copy-start.1 = (f32[3,8,64,256]{3,2,1,0:T(8,128)S(1)}, f32[3,8,64,256]{3,2,1,0:T(8,128)}, u32[]{:S(2)}) copy-start(f32[3,8,64,256]{3,2,1,0:T(8,128)} %state.5) | copy-start | bytes 4718596
  11.8 16.0 %copy-start.4 = (bf16[3,8192]{1,0:T(4,128)(2,1)S(1)}, bf16[3,8192]{1,0:T(4,128)(2,1)}, u32[]{:S(2)}) copy-start(bf16[3,8192]{1,0:T(4,128)(2,1)} %q2.3) | copy-start | bytes 147460
  11.8 16.0 %copy-start.9 = (bf16[3,8192]{1,0:T(4,128)(2,1)S(1)}, bf16[3,8192]{1,0:T(4,128)(2,1)}, u32[]{:S(2)}) copy-start(bf16[3,8192]{1,0:T(4,128)(2,1)} %q1.1) | copy-start | bytes 147460
  11.8 16.0 %copy-start.11 = (bf16[3,2048]{1,0:T(4,128)(2,1)S(1)}, bf16[3,2048]{1,0:T(4,128)(2,1)}, u32[]{:S(2)}) copy-start(bf16[3,2048]{1,0:T(4,128)(2,1)} %kv2.3) | copy-start | bytes 36868
  11.8 16.0 %copy-start.15 = (bf16[3,512]{1,0:T(4,128)(2,1)S(1)}, bf16[3,512]{1,0:T(4,128)(2,1)}, u32[]{:S(2)}) copy-start(bf16[3,512]{1,0:T(4,128)(2,1)} %x2.5) | copy-start | bytes 9220
  11.8 16.0 %copy-start.17 = (bf16[3,1024]{1,0:T(4,128)(2,1)S(1)}, bf16[3,1024]{1,0:T(4,128)(2,1)}, u32[]{:S(2)}) copy-start(bf16[3,1024]{1,0:T(4,128)(2,1)} %c2.3) | copy-start | bytes 18436
  11.8 16.0 %copy-start.18 = (bf16[3,2048]{1,0:T(4,128)(2,1)S(1)}, bf16[3,2048]{1,0:T(4,128)(2,1)}, u32[]{:S(2)}) copy-start(bf16[3,2048]{1,0:T(4,128)(2,1)} %kv1.1) | copy-start | bytes 36868
  11.9 16.0 %copy-start.20 = (bf16[3,512]{1,0:T(4,128)(2,1)S(1)}, bf16[3,512]{1,0:T(4,128)(2,1)}, u32[]{:S(2)}) copy-start(bf16[3,512]{1,0:T(4,128)(2,1)} %z2.3) | copy-start | bytes 9220
  11.9 16.0 %copy-start.25 = (bf16[3,1024]{1,0:T(4,128)(2,1)S(1)}, bf16[3,1024]{1,0:T(4,128)(2,1)}, u32[]{:S(2)}) copy-start(bf16[3,1024]{1,0:T(4,128)(2,1)} %c1.1) | copy-start | bytes 18436
  11.9 16.0 %copy-start.26 = (bf16[3,512]{1,0:T(4,128)(2,1)S(1)}, bf16[3,512]{1,0:T(4,128)(2,1)}, u32[]{:S(2)}) copy-start(bf16[3,512]{1,0:T(4,128)(2,1)} %z1.1) | copy-start | bytes 9220
  11.9 16.0 %copy-start.27 = (s32[3,4]{1,0:T(4,128)S(1)}, s32[3,4]{1,0:T(4,128)}, u32[]{:S(2)}) copy-start(s32[3,4]{1,0:T(4,128)} %table.1) | copy-start | bytes 148
  11.9 16.0 %copy-start.29 = (f32[8]{0:T(128)S(1)}, f32[8]{0:T(128)}, u32[]{:S(2)}) copy-start(f32[8]{0:T(128)} %param.98) | copy-start | bytes 100
  11.9 16.0 %copy-start.31 = (s32[96]{0:T(128)S(1)}, s32[96]{0:T(128)}, u32[]{:S(2)}) copy-start(s32[96]{0:T(128)} %lens.1) | copy-start | bytes 1156
  11.9 16.0 %copy-start.32 = (f32[8]{0:T(128)S(1)}, f32[8]{0:T(128)}, u32[]{:S(2)}) copy-start(f32[8]{0:T(128)} %param.99) | copy-start | bytes 100
  13.0 14.7 %collective-permute-start.24 = (bf16[2,6656]{1,0:T(2,128)(2,1)S(1)}, bf16[2,6656]{1,0:T(2,128)(2,1)}, u32[]{:S(2)}, u32[]{:S(2)}) collective-permute-start(bf16[2,6656]{1,0:T(2,128)(2,1)S(1)} %param.24), channel_id=1, source_target_pairs={{0,400},{1,401},{2,402},{3,403},{4,404},{5,405},{6,406},{7,407},{8... | collective-permute-start | bytes 79880 | tf_op jit(solution)/shard_map/cond/branch_24_fun/ppermute | solution.py:480
  27.9 1.1 copy-start.2
  29.1 73.6 %copy-start.30 = (f32[512]{0:T(512)S(1)}, f32[512]{0:T(512)}, u32[]{:S(2)}) copy-start(f32[512]{0:T(512)} %param.100) | copy-start | bytes 6148
  46.1 56.5 %collective-permute-start.127 = (bf16[8,64,256]{2,1,0:T(8,128)(2,1)S(1)}, bf16[8,64,256]{2,1,0:T(8,128)(2,1)}, u32[]{:S(2)}, u32[]{:S(2)}) collective-permute-start(bf16[8,64,256]{2,1,0:T(8,128)(2,1)S(1)} %get-tuple-element.321), channel_id=1, source_target_pairs={{0,400},{1,401},{2,402},{3,403},{4,404},{5,405},{6,406},{7,407},{8... | collective-permute-start | bytes 786440 | tf_op jit(solution)/shard_map/cond/branch_24_fun/ppermute | solution.py:484
  55.0 47.6 %collective-permute-start.128 = (bf16[64,128]{1,0:T(8,128)(2,1)S(1)}, bf16[64,128]{1,0:T(8,128)(2,1)}, u32[]{:S(2)}, u32[]{:S(2)}) collective-permute-start(bf16[64,128]{1,0:T(8,128)(2,1)S(1)} %get-tuple-element.322), channel_id=1, source_target_pairs={{0,2},{1,3},{2,0},{3,1},{4,6},{5,7},{6,4},{7,5},{8,10},{9,11},{10,... | collective-permute-start | bytes 49160 | tf_op jit(solution)/shard_map/cond/branch_24_fun/ppermute | solution.py:485
  63.8 29.6 %collective-permute-start.129 = (bf16[32,128]{1,0:T(8,128)(2,1)S(1)}, bf16[32,128]{1,0:T(8,128)(2,1)}, u32[]{:S(2)}, u32[]{:S(2)}) collective-permute-start(bf16[32,128]{1,0:T(8,128)(2,1)S(1)} %get-tuple-element.323), channel_id=1, source_target_pairs={{0,400},{1,401},{2,402},{3,403},{4,404},{5,405},{6,406},{7,407},{8... | collective-permute-start | bytes 24584 | tf_op jit(solution)/shard_map/cond/branch_24_fun/ppermute | solution.py:487
  74.4 28.2 %collective-permute-start.130 = (bf16[32,128]{1,0:T(8,128)(2,1)S(1)}, bf16[32,128]{1,0:T(8,128)(2,1)}, u32[]{:S(2)}, u32[]{:S(2)}) collective-permute-start(bf16[32,128]{1,0:T(8,128)(2,1)S(1)} %get-tuple-element.323), channel_id=1, source_target_pairs={{0,402},{1,403},{2,400},{3,401},{4,406},{5,407},{6,404},{7,405},{8... | collective-permute-start | bytes 24584 | tf_op jit(solution)/shard_map/cond/branch_24_fun/ppermute | solution.py:486
  104.2 10.8 %all-to-all-start.1 = ((bf16[8,64,128]{2,1,0:T(8,128)(2,1)}), bf16[8,64,128]{2,1,0:T(8,128)(2,1)S(1)}, u32[]{:S(2)}, u32[]{:S(2)}) async-start(bf16[8,64,128]{2,1,0:T(8,128)(2,1)} %get-tuple-element.372), calls=%async_computation.1 | async-start | bytes 262144 | tf_op jit(solution)/shard_map/all_to_all | solution.py:470
  (7 other events, 4.8 us)

commit v2 on v1

v2 whole, which is shorter than its diff:
```python
import functools

import jax
import jax.numpy as jnp
from jax import lax
from jax.experimental import pallas as pl
from jax.experimental.pallas import tpu as pltpu
from jax.sharding import PartitionSpec as P

F32 = jnp.float32
BF16 = jnp.bfloat16
I32 = jnp.int32

HPG = 32
QDIM = 128
STATE = 256
REQ = 3
HEADS = 8
HALF = HEADS // 2
HDIM = 64
COLS = HEADS * HDIM
STATE_ROWS = HALF * HDIM * 2
KVHEADS = 8
QPK = 8
QHEADS = KVHEADS * QPK
KVW = 2 * KVHEADS * QDIM
PAGE = 16
POOL = 12
PP = 4
SPAN = PP * PAGE
KEYS = POOL * PAGE
EXTRA = 16
NORM = HPG * HDIM
NEG = -1e30
SCALE = 1.0 / QDIM**0.5

KV = QHEADS
X2 = KV + 16
Z2 = X2 + 4
B2 = Z2 + 4
C2 = B2 + 2
D2 = C2 + 2
D1 = D2 + 1
X1 = D1 + 1
B1 = X1 + 4
SWAP = 112

LSE = QHEADS
GHI = LSE + 8
GLO = GHI + 4
MOVED = 80

VMEM = pltpu.VMEM
NT = (((1,), (1,)), ((), ()))


def iota(shape, dim):
    return lax.broadcasted_iota(I32, shape, dim)


def split3(v):
    a = v.astype(BF16).astype(F32)
    rest = v - a
    b = rest.astype(BF16).astype(F32)
    c = (rest - b).astype(BF16).astype(F32)
    return a, b, c


def store_states(out, at, v):
    n = HALF * HDIM
    v = v.reshape(n, STATE).astype(BF16)
    out[at : at + n, :] = v[:, :128]
    out[at + n : at + 2 * n, :] = v[:, 128:]


def load_state(ref, at, h):
    first = at + h * HDIM
    second = first + HALF * HDIM
    return jnp.concatenate([ref[first : first + HDIM, :], ref[second : second + HDIM, :]], axis=1)


def slot_of(mig):
    inst = lax.axis_index("inst")
    return mig[inst, 0] - inst * REQ


def whole(a):
    return pl.BlockSpec(a.shape, lambda i: (0,) * a.ndim)


def here(n):
    return [pl.BlockSpec(memory_space=VMEM)] * n


def scalars(n):
    return [pl.BlockSpec(memory_space=pltpu.SMEM)] * n


def call(body, out_shape, in_specs, out_specs, scratch=(), grid=(1,), **kw):
    return pl.pallas_call(
        body,
        out_shape=out_shape,
        in_specs=in_specs,
        out_specs=out_specs,
        scratch_shapes=list(scratch),
        compiler_params=pltpu.CompilerParams(vmem_limit_bytes=60 * 2**20),
        grid=grid,
        **kw,
    )


def like(*shape, dtype=BF16):
    return jax.ShapeDtypeStruct(shape, dtype)


def expand(per_head, rows):
    head = iota((rows, COLS), 1) // HDIM
    out = jnp.zeros((rows, COLS), F32)
    for h in range(HEADS):
        out = jnp.where(head == h, per_head[:, h : h + 1], out)
    return out


def flat(rows):
    return jnp.concatenate([rows[k : k + 1] for k in range(rows.shape[0])], axis=1)


def softplus(v):
    return jnp.maximum(v, 0.0) + jnp.log1p(jnp.exp(-jnp.abs(v)))


def silu(v):
    return v / (1.0 + jnp.exp(-v))


def group_cols():
    g = lax.axis_index("tp") * HEADS // HPG
    return pl.ds(pl.multiple_of(g * STATE, STATE), STATE)


def hi_lo(v):
    hi = v.astype(BF16)
    return hi, (v - hi.astype(F32)).astype(BF16)


def prepare_body(mig, x1, dt1, b1, q2, kv2, x2, z2, dt2, b2, c2, state, out, rows, held, sem):
    slot = slot_of(mig)
    copy = pltpu.make_async_copy(state.at[slot, :HALF], held, sem)
    copy.start()

    def put(at, v):
        v = v.astype(F32)
        v = jnp.sum(jnp.where(iota(v.shape, 0) == slot, v, 0.0), axis=0, keepdims=True)
        width = min(v.shape[1], 128)
        for k in range(v.shape[1] // width):
            rows[at + k : at + k + 1, :width] = v[:, k * width : (k + 1) * width]

    cols = group_cols()
    rows[D2:, :] = jnp.zeros_like(rows[D2:, :])
    put(0, q2[...])
    put(KV, kv2[...])
    put(X2, x2[...])
    put(Z2, z2[...])
    put(B2, b2[:, cols])
    put(C2, c2[:, cols])
    put(D2, dt2[...])
    put(D1, dt1[...])
    put(X1, x1[...])
    put(B1, b1[:, cols])
    out[:SWAP, :] = rows[...].astype(BF16)
    copy.wait()
    store_states(out, SWAP, held[...])


def prepare(mig, *rest):
    return call(
        prepare_body,
        like(SWAP + STATE_ROWS, 128),
        scalars(1) + [whole(a) for a in rest[:-1]] + [pl.BlockSpec(memory_space=pl.ANY)],
        here(1)[0],
        [VMEM((SWAP, 128), F32), VMEM((HALF, HDIM, STATE), F32), pltpu.SemaphoreType.DMA],
        name="prepare",
    )(mig, *rest)


def stats_row(col, sub, lane):
    a, b, c = split3(jnp.broadcast_to(col, col.shape[:2] + (128,)))
    row = jnp.where(
        lane == sub,
        a,
        jnp.where(lane == sub + 8, b, jnp.where(lane == sub + 16, c, 0.0)),
    )
    return jnp.sum(row, axis=1, keepdims=True)


def stats_col(row, sub, lane):
    spread = jnp.broadcast_to(row, (row.shape[0], 8, 128))
    mine = jnp.logical_and(lane < 24, lane % 8 == sub)
    return jnp.sum(jnp.where(mine, spread, 0.0), axis=2, keepdims=True)


def partial_body(
    mig, lens, table, swapped, x1, z1, dt1, b1, c1, q1, kv1, state, cache,
    rate, bias, skip, x2, z2, dt2, b2, c2, q2, kv2,
    blocks, gated, leaving,
    q8, kv16, x8, z8, d8, b8, c8, scr,
):
    slot = slot_of(mig)
    inst = lax.axis_index("inst")
    tp = lax.axis_index("tp")
    cols = group_cols()
    sw = swapped[:SWAP, :].astype(F32)

    def rows8(scr, one, two, moved):
        n = one.shape[-1]
        scr[...] = jnp.zeros_like(scr)
        scr[0:3, :n] = one.astype(F32)
        scr[3:6, :n] = jnp.where(iota((3, n), 0) == slot, moved, two.astype(F32))
        return scr[...]

    q8[6:8, :] = jnp.zeros_like(q8[6:8, :])
    q8[0:3, :] = q1[...].astype(F32)
    q8[3:6, :] = q2[...].astype(F32)
    rows3 = iota((3, 128), 0) == slot
    for a in range(QHEADS):
        at = slice(a * QDIM, (a + 1) * QDIM)
        q8[3:6, at] = jnp.where(rows3, sw[a : a + 1], q8[3:6, at])
    kv16[...] = jnp.zeros_like(kv16)
    kv16[0:3, :] = kv1[...].astype(F32)
    kv16[3:6, :] = kv2[...].astype(F32)
    for a in range(2 * KVHEADS):
        at = slice(a * QDIM, (a + 1) * QDIM)
        kv16[3:6, at] = jnp.where(rows3, sw[KV + a : KV + a + 1], kv16[3:6, at])

    xx = rows8(x8, x1[...], x2[...], flat(sw[X2 : X2 + 4]))
    zz = rows8(z8, z1[...], z2[...], flat(sw[Z2 : Z2 + 4]))
    bb = rows8(b8, b1[:, cols], b2[:, cols], flat(sw[B2 : B2 + 2]))
    cc = rows8(c8, c1[:, cols], c2[:, cols], flat(sw[C2 : C2 + 2]))
    dd = rows8(d8, dt1[...], dt2[...], sw[D2 : D2 + 1, :HEADS])
    dt = softplus(expand(dd, 8) + expand(bias[...], 1))
    decay = jnp.exp(-dt * expand(rate[...], 1))
    read = jnp.zeros((8, COLS), F32)
    row256 = iota((8, STATE), 0)
    for r in range(REQ):
        ch = jnp.where(jnp.logical_or(row256 == r, row256 == r + 3), cc, 0.0).astype(BF16)
        for part in hi_lo(state[r].reshape(COLS, STATE)):
            read += lax.dot_general(ch, part, NT, preferred_element_type=F32)
    store_states(leaving, MOVED, state[slot, HALF:])
    pushed = dt * xx
    same = jnp.sum(bb * cc, axis=1, keepdims=True)
    cross = jnp.sum(pltpu.roll(bb, 3, 0) * cc, axis=1, keepdims=True)
    first = pltpu.roll(decay, 3, 0) * read + pltpu.roll(pushed, 3, 0) * cross
    row = iota((8, COLS), 0)
    y = decay * jnp.where(row >= 3, first, read) + pushed * same + expand(skip[...], 1) * xx
    g = y * silu(zz)
    gated[...] = g
    g = jnp.sum(jnp.where(row == slot + 3, g, 0.0), axis=0, keepdims=True)
    hi = g.astype(BF16).astype(F32)
    for k in range(4):
        piece = slice(k * 128, (k + 1) * 128)
        scr[GHI + k : GHI + k + 1, :] = hi[:, piece]
        scr[GLO + k : GLO + k + 1, :] = (g - hi)[:, piece]

    lane = iota((1, KEYS + EXTRA), 1)
    owner = jnp.full(lane.shape, -1, I32)
    ok = jnp.zeros(lane.shape, I32)
    late = jnp.logical_and(lane >= KEYS + REQ, lane < KEYS + 2 * REQ)
    for r in range(REQ):
        length = lens[inst * REQ + r]
        for p in range(PP):
            at = (lane // PAGE) == table[r, p]
            pos = tp * SPAN + p * PAGE + lane % PAGE
            owner = jnp.where(at, r, owner)
            ok = jnp.where(jnp.logical_and(at, pos < length), 1, ok)
        for e, pos in ((r, length), (r + REQ, length + 1)):
            at = lane == KEYS + e
            owner = jnp.where(at, r, owner)
            ok = jnp.where(jnp.logical_and(at, pos // SPAN == tp), 1, ok)
    row = iota((8, KEYS + EXTRA), 0)
    mine = jnp.where(row < 3, row, jnp.where(row < 6, row - 3, -2))
    valid = (mine == owner) & (ok == 1) & ((row >= 3) | jnp.logical_not(late))
    valid = jnp.broadcast_to(valid.astype(F32)[None], (QPK, 8, KEYS + EXTRA)) > 0.0
    sub = iota((QPK, 8, 128), 1)
    lane3 = iota((QPK, 8, 128), 2)
    lane2 = iota((QPK, 128), 1)
    extra = kv16[...].astype(BF16)
    stats = jnp.zeros((QPK, 128), F32)
    for k in range(KVHEADS):
        qk = jnp.concatenate(
            [q8[:, (k * QPK + h) * QDIM : (k * QPK + h + 1) * QDIM] for h in range(QPK)], axis=0
        ).astype(BF16)
        kcols = slice(k * QDIM, (k + 1) * QDIM)
        vcols = slice((KVHEADS + k) * QDIM, (KVHEADS + k + 1) * QDIM)
        keys = jnp.concatenate([cache[:, :, kcols].reshape(KEYS, QDIM), extra[:, kcols]], axis=0)
        vals = jnp.concatenate([cache[:, :, vcols].reshape(KEYS, QDIM), extra[:, vcols]], axis=0)
        s = lax.dot_general(qk, keys, NT, preferred_element_type=F32) * SCALE
        s = jnp.where(valid, s.reshape(QPK, 8, KEYS + EXTRA), NEG)
        top = jnp.max(s, axis=2, keepdims=True)
        w = jnp.where(valid, jnp.exp(s - top), 0.0).astype(BF16)
        total = jnp.sum(w.astype(F32), axis=2, keepdims=True)
        acc = jnp.dot(w.reshape(QPK * 8, KEYS + EXTRA), vals, preferred_element_type=F32)
        some = total > 0.0
        safe = jnp.where(some, total, 1.0)
        lse = jnp.where(some, top + jnp.log(safe), NEG)
        o = acc.reshape(QPK, 8, QDIM) / safe
        out = jnp.where(sub == 6, stats_row(lse, sub, lane3), o)
        blocks[k] = out.reshape(QPK * 8, QDIM).astype(BF16)
        gone = sub == slot + 3
        scr[k * QPK : (k + 1) * QPK, :] = jnp.sum(jnp.where(gone, o, 0.0), axis=1)
        a, b, c = split3(jnp.sum(jnp.where(gone, lse, 0.0), axis=1))
        stats = jnp.where(lane2 == 3 * k, a, stats)
        stats = jnp.where(lane2 == 3 * k + 1, b, stats)
        stats = jnp.where(lane2 == 3 * k + 2, c, stats)
    scr[LSE : LSE + QPK, :] = stats
    leaving[:MOVED, :] = scr[...].astype(BF16)


def partials(mig, lens, table, swapped, *rest):
    return call(
        partial_body,
        (
            like(KVHEADS, QPK * 8, QDIM),
            like(8, COLS, dtype=F32),
            like(MOVED + STATE_ROWS, 128),
        ),
        scalars(3) + here(1) + [whole(a) for a in rest],
        tuple(here(3)),
        [
            VMEM((8, QHEADS * QDIM), F32),
            VMEM((EXTRA, KVW), F32),
            VMEM((8, COLS), F32),
            VMEM((8, COLS), F32),
            VMEM((8, 128), F32),
            VMEM((8, STATE), F32),
            VMEM((8, STATE), F32),
            VMEM((MOVED, 128), F32),
        ],
        name="partials",
    )(mig, lens, table, swapped, *rest)


def insert_body(mig, blocks, gated, moved, out, gated_out):
    slot = slot_of(mig)
    sub = iota((QPK, 8, 128), 1)
    lane = iota((QPK, 8, 128), 2)
    mv = moved[:MOVED, :].astype(F32)
    g = flat(mv[GHI : GHI + 4] + mv[GLO : GLO + 4])
    g = jnp.where(iota((8, COLS), 0) == slot + 3, g, gated[...])
    gated_out[...] = g
    squares = jnp.sum(g * g, axis=1, keepdims=True)
    sq_row = stats_row(squares[None], sub[:1], lane[:1])
    stats = mv[LSE : LSE + QPK]
    lane2 = iota((QPK, 128), 1)
    mine = jnp.logical_and(lane < 24, lane % 8 == slot + 3)
    for k in range(KVHEADS):
        lse = jnp.where(lane2 // 3 == k, stats, 0.0)
        lse = jnp.sum(lse, axis=1, keepdims=True)[:, None, :]
        a, b, c = split3(jnp.broadcast_to(lse, (QPK, 8, 128)))
        terms = jnp.where(lane < 8, a, jnp.where(lane < 16, b, c))
        v = blocks[k].astype(F32).reshape(QPK, 8, 128)
        v = jnp.where(sub == slot + 3, mv[k * QPK : (k + 1) * QPK][:, None, :], v)
        v = jnp.where(jnp.logical_and(sub == 6, mine), terms, v)
        v = jnp.where(sub == 7, sq_row, v)
        v = v.reshape(QPK * 8, 128).astype(BF16)
        for z in range(2):
            out[k // 2 * 4 + z * 2 + k % 2] = v


def insert(mig, blocks, gated, moved):
    return call(
        insert_body,
        (like(2 * KVHEADS, QPK * 8, QDIM), like(8, COLS, dtype=F32)),
        scalars(1) + here(3),
        tuple(here(2)),
        name="insert",
    )(mig, blocks, gated, moved)


def finish_body(recv, gated, gain, blocks, m1, m2, scr):
    x = lax.axis_index("tp") // 4
    sub = iota((QPK, 8, 128), 1)
    lane = iota((QPK, 8, 128), 2)
    n = recv.shape[0]
    lses = [stats_col(recv[j].astype(F32).reshape(QPK, 8, 128)[:, 6:7], sub, lane) for j in range(n)]
    top = functools.reduce(jnp.maximum, lses)
    total = jnp.zeros_like(top)
    acc = jnp.zeros((QPK, 8, 128), F32)
    for j in range(n):
        w = jnp.exp(lses[j] - top)
        total += w
        acc += w * recv[j].astype(F32).reshape(QPK, 8, 128)
    o = (acc / total).reshape(QPK * 8, 128).astype(BF16)
    for k in range(KVHEADS):
        blocks[k] = o

    rows = recv[4 * x].astype(F32)[7:8]
    for j in range(1, 4):
        rows += recv[4 * x + j].astype(F32)[7:8]
    squares = stats_col(rows[None], sub[:1], lane[:1])[0]
    scr[...] = gated[...] * lax.rsqrt(squares * (1.0 / NORM) + 1e-05) * gain[...]
    m1[...] = scr[0:3, :].astype(BF16)
    m2[...] = scr[3:6, :].astype(BF16)


def finish(recv, gated, gain):
    return call(
        finish_body,
        (like(KVHEADS, QPK * 8, 128), like(REQ, COLS), like(REQ, COLS)),
        here(2) + [whole(gain)],
        tuple(here(3)),
        [VMEM((8, COLS), F32)],
        name="finish",
    )(recv, gated, gain)


def spread_body(recv, a1, a2, scr):
    for k in range(KVHEADS):
        rows = recv[k].astype(F32)
        for h in range(QPK):
            at = (k * QPK + h) * QDIM
            scr[:, at : at + QDIM] = rows[h * 8 : (h + 1) * 8]
    a1[...] = scr[0:3, :].astype(BF16)
    a2[...] = scr[3:6, :].astype(BF16)


def spread(recv):
    n = QHEADS * QDIM
    return call(
        spread_body,
        (like(REQ, n),) * 2,
        here(1),
        tuple(here(2)),
        [VMEM((8, n), F32)],
        name="spread",
    )(recv)


def update_body(mig, swapped, moved, x1, dt1, b1, rate, bias, x2, dt2, b2, state, out, x8, d8, b8):
    slot = slot_of(mig)
    r = pl.program_id(0)
    cols = group_cols()
    sw = swapped[:SWAP, :].astype(F32)

    def rows8(scr, one, two, moved):
        n = one.shape[-1]
        scr[...] = jnp.zeros_like(scr)
        scr[0:3, :n] = jnp.where(iota((3, n), 0) == slot, moved, one.astype(F32))
        scr[3:6, :n] = two.astype(F32)
        return scr[...]

    xx = rows8(x8, x1[...], x2[...], flat(sw[X1 : X1 + 4]))
    bb = rows8(b8, b1[:, cols], b2[:, cols], flat(sw[B1 : B1 + 2]))
    dd = rows8(d8, dt1[...], dt2[...], sw[D1 : D1 + 1, :HEADS])
    dt = softplus(expand(dd, 8) + expand(bias[...], 1))
    decay = jnp.exp(-dt * expand(rate[...], 1))
    pushed = dt * xx
    later = pltpu.roll(decay, 5, 0)
    row = iota((8, COLS), 0)
    u = jnp.where(row < 3, pushed * later, pushed)
    both = jnp.sum(jnp.where(row == r, decay * later, 0.0), axis=0, keepdims=True)
    mine = jnp.logical_or(row == r, row == r + 3)
    bh = bb.astype(BF16)
    add = jnp.zeros((COLS, STATE), F32)
    for part in hi_lo(jnp.where(mine, u, 0.0)):
        add += lax.dot_general(part, bh, (((0,), (0,)), ((), ())), preferred_element_type=F32)
    new = r == slot
    for h in range(HEADS):
        if h < HALF:
            arrived = load_state(swapped, SWAP, h)
        else:
            arrived = load_state(moved, MOVED, h - HALF)
        s = jnp.where(new, arrived.astype(F32), state[0, h])
        d = both[:, h * HDIM : h * HDIM + 1]
        out[0, h] = d * s + add[h * HDIM : (h + 1) * HDIM]


def update(mig, swapped, moved, *rest):
    state = rest[-1]
    block = pl.BlockSpec((1,) + state.shape[1:], lambda r: (r, 0, 0, 0))
    return call(
        update_body,
        like(*state.shape, dtype=F32),
        scalars(1) + here(2) + [whole(a) for a in rest[:-1]] + [block],
        block,
        [VMEM((8, COLS), F32), VMEM((8, 128), F32), VMEM((8, STATE), F32)],
        grid=(REQ,),
        name="update",
    )(mig, swapped, moved, *rest)


PLANE = [[x * 4 + z * 2 + c for x in range(4) for c in range(2)] for z in range(2)]


def swap(m, v):
    return lax.ppermute(v, "inst", [(s, s ^ m) for s in range(lax.axis_size("inst"))])


def shards(
    x_one, z_one, dt_one, b_one, c_one, q_one, kv_one, state, cache, page_table,
    lengths, migration, decay_rate, dt_bias, skip_gain, norm_gain,
    x_two, z_two, dt_two, b_two, c_two, q_two, kv_two,
):
    rate, bias, skip, gain = decay_rate[None], dt_bias[None], skip_gain[None], norm_gain[None]
    which = migration[0, 1] - 1

    def by_partner(body, *operands):
        ways = range(1, lax.axis_size("inst"))
        return lax.switch(which, [functools.partial(body, m) for m in ways], *operands)

    payload = prepare(
        migration, x_one, dt_one, b_one, q_two, kv_two, x_two, z_two, dt_two, b_two, c_two, state
    )
    swapped = by_partner(swap, payload)
    blocks, gated, leaving = partials(
        migration, lengths, page_table, swapped,
        x_one, z_one, dt_one, b_one, c_one, q_one, kv_one, state, cache,
        rate, bias, skip, x_two, z_two, dt_two, b_two, c_two, q_two, kv_two,
    )
    moved = by_partner(swap, leaving)
    blocks, gated = insert(migration, blocks, gated, moved)
    recv = lax.all_to_all(blocks, "tp", 0, 0)
    blocks, mamba_one, mamba_two = finish(recv, gated, gain)
    recv = lax.all_to_all(blocks, "tp", 0, 0, axis_index_groups=PLANE)
    attn_one, attn_two = spread(recv)
    state_out = update(
        migration, swapped, moved, x_one, dt_one, b_one, rate, bias, x_two, dt_two, b_two, state
    )
    return mamba_one, attn_one, mamba_two, attn_two, state_out


def solution(mesh):
    row = P("inst", "tp")
    wide = P("inst", None)
    head = P("tp")
    states = P("inst", "tp", None, None)
    return jax.shard_map(
        shards,
        mesh=mesh,
        in_specs=(
            row, row, row, wide, wide, wide, wide, states, P("inst", None, "tp"), row,
            P(), P(), head, head, head, head, row, row, row, wide, wide, wide, wide,
        ),
        out_specs=(row, wide, row, wide, states),
        check_vma=False,
    )
```

time: 117 us -> 104 us (0.89)
  the two profiles are of different devices: /device:TPU:1 before, /device:TPU:56 now
where the time goes in v2:
time: 104 us; the launch traced here: 103 us
  blocking collectives  34.1 us (33%)
  waiting for transfers between devices  34 us (33%)
  Pallas kernels  17.5 us (17%)
  starting transfers between devices  13 us (12%)
  local copies, waits for them, and re-layouts  3.21 us (3%)
  between operations  1.31 us (1%)
    all_to_all x1, blocking collectives, shards(): recv = lax.all_to_all(blocks, 'tp', 0, 0)  34.1 us
    ppermute x2, waiting for transfers between devices, swap(): lax.ppermute(v, 'inst', [(s, s ^ m) for s in range(lax.axis_size('inst'))])  32.2 us
    ppermute x2, starting transfers between devices, swap(): lax.ppermute(v, 'inst', [(s, s ^ m) for s in range(lax.axis_size('inst'))])  9.67 us
    pallas_call x1, Pallas kernels, partials(): call(partial_body, (like(KVHEADS, QPK * 8, QDIM), like(8, COLS, dtype=F32...  5.57 us
    pallas_call x1, Pallas kernels, update(): call(update_body, like(*state.shape, dtype=F32), scalars(1) + here(2) + [...  4.27 us
    all_to_all x1, starting transfers between devices, shards(): recv = lax.all_to_all(blocks, 'tp', 0, 0, axis_index_groups=PLANE)  3.37 us
  transfers between devices with their start and end apart: 3, of which 3 were waited for; matrix products, arithmetic and copies ran while one was open for 0% of the time, Pallas kernels for 4%

profile of v2, /device:TPU:56, one launch (start us, length us, event | category | flops | bytes accessed | tf_op | source)
XLA Modules:
  0.0 103.2 jit_solution(7399750582949267116)
XLA Ops:
  0.6 1.2 %slice.3 = s32[1,1]{0,1:T(1,128)} slice(s32[32,2]{0,1:T(2,128)} %param.96), slice={[0:1], [1:2]} | slice | bytes 8 | tf_op jit(solution)/shard_map/slice | solution.py:504
  1.8 1.4 %copy.30.mig = s32[32,2]{1,0:T(8,128)} copy(s32[32,2]{0,1:T(2,128)} %param.96) | data formatting | bytes 512 | tf_op args[11]
  3.8 2.1 %prepare.1 = bf16[624,128]{1,0:T(8,128)(2,1)S(1)} custom-call(s32[32,2]{1,0:T(8,128)} %copy.30.mig, bf16[3,512]{1,0:T(4,128)(2,1)} %x1.5, bf16[3,8]{1,0:T(4,128)(2,1)} %dt1.5, bf16[3,1024]{1,0:T(4,128)(2,1)} %b1.5, bf16[3,8192]{1,0:T(4,128)(2,1)} %q2.3, bf16[3,2048]{1,0:T(4,128)(2,1)} %kv2.3, bf16[3,512]{1,0:T(4,128)(2,1)} %x2.5, bf16[3,512]{1,0:T(4,128)(2,1)} %z2.3, ...), custom_call_target="tpu_custom_call" | custom-call | tf_op jit(solution)/shard_map/prepare/pallas_call | solution.py:176
  5.9 22.3 %conditional.2 = (bf16[624,128]{1,0:T(8,128)(2,1)}) conditional(s32[]{:T(128)} %bitcast, bf16[624,128]{1,0:T(8,128)(2,1)S(1)} %prepare.1, bf16[624,128]{1,0:T(8,128)(2,1)S(1)} %prepare.1, bf16[624,128]{1,0:T(8,128)(2,1)S(1)} %prepare.1, bf16[624,128]{1,0:T(8,128)(2,1)S(1)} %prepare.1, ...), branch_computations={%region_0.0_spmd, %region_1.0_spmd, %region_2.0_spmd, %region_3.0_... | conditional | bytes 639024 | solution.py:508
  5.9 7.7 %collective-permute-start.19 = (bf16[624,128]{1,0:T(8,128)(2,1)S(1)}, bf16[624,128]{1,0:T(8,128)(2,1)}, u32[]{:S(2)}, u32[]{:S(2)}) collective-permute-start(bf16[624,128]{1,0:T(8,128)(2,1)S(1)} %param.19), channel_id=1, source_target_pairs={{0,320},{16,336},{32,352},{48,368},{64,256},{80,272},{96,288},{112... | collective-permute-start | bytes 479240 | tf_op jit(solution)/shard_map/cond/branch_19_fun/ppermute | solution.py:495
  13.7 14.5 %collective-permute-done.19 = bf16[624,128]{1,0:T(8,128)(2,1)} collective-permute-done((bf16[624,128]{1,0:T(8,128)(2,1)S(1)}, bf16[624,128]{1,0:T(8,128)(2,1)}, u32[]{:S(2)}, u32[]{:S(2)}) %collective-permute-start.19) | collective-permute-done | bytes 159776 | tf_op jit(solution)/shard_map/cond/branch_19_fun/ppermute | solution.py:495
  28.2 5.6 %partials.1 = (bf16[8,64,128]{2,1,0:T(8,128)(2,1)}, f32[8,512]{1,0:T(8,128)}, bf16[592,128]{1,0:T(8,128)(2,1)S(1)}) custom-call(s32[32,2]{1,0:T(8,128)} %copy.30.mig, s32[96]{0:T(128)} %lens.1, s32[3,4]{1,0:T(4,128)} %table.1, bf16[624,128]{1,0:T(8,128)(2,1)} %get-tuple-element.151.swapped, bf16[3,512]{1,0:T(4,128)(2,1)} %x1.5, bf16[3,512]{1,0:T(4,128)(2,1)} %z1.1, ...), custom_call_target="tpu_custom_call" | custom-call | tf_op jit(solution)/shard_map/partials/pallas_call | solution.py:319
  33.7 19.7 %conditional.3 = (bf16[592,128]{1,0:T(8,128)(2,1)}) conditional(s32[]{:T(128)} %bitcast, bf16[592,128]{1,0:T(8,128)(2,1)S(1)} %get-tuple-element.143, bf16[592,128]{1,0:T(8,128)(2,1)S(1)} %get-tuple-element.143, bf16[592,128]{1,0:T(8,128)(2,1)S(1)} %get-tuple-element.143, ...), branch_computations={%region_31.0_spmd, %region_32.0_spmd, %region_33.0_spmd, %region_3... | conditional | bytes 606256 | solution.py:508
  33.8 1.9 %collective-permute-start.50 = (bf16[592,128]{1,0:T(8,128)(2,1)S(1)}, bf16[592,128]{1,0:T(8,128)(2,1)}, u32[]{:S(2)}, u32[]{:S(2)}) collective-permute-start(bf16[592,128]{1,0:T(8,128)(2,1)S(1)} %param.50), channel_id=1, source_target_pairs={{0,320},{16,336},{32,352},{48,368},{64,256},{80,272},{96,288},{112... | collective-permute-start | bytes 454664 | tf_op jit(solution)/shard_map/cond/branch_19_fun/ppermute | solution.py:495
  35.7 17.7 %collective-permute-done.50 = bf16[592,128]{1,0:T(8,128)(2,1)} collective-permute-done((bf16[592,128]{1,0:T(8,128)(2,1)S(1)}, bf16[592,128]{1,0:T(8,128)(2,1)}, u32[]{:S(2)}, u32[]{:S(2)}) %collective-permute-start.50) | collective-permute-done | bytes 151584 | tf_op jit(solution)/shard_map/cond/branch_19_fun/ppermute | solution.py:495
  53.4 2.0 %insert.1 = (bf16[16,64,128]{2,1,0:T(8,128)(2,1)}, f32[8,512]{1,0:T(8,128)}) custom-call(s32[32,2]{1,0:T(8,128)} %copy.30.mig, bf16[8,64,128]{2,1,0:T(8,128)(2,1)} %get-tuple-element.141.blocks, f32[8,512]{1,0:T(8,128)} %get-tuple-element.142.gated, bf16[592,128]{1,0:T(8,128)(2,1)} %get-tuple-element.152.moved), custom_call_target="tpu_custom_call" | custom-call | tf_op jit(solution)/shard_map/insert/pallas_call | solution.py:370
  55.4 34.1 %all_to_all.10.recv = bf16[16,64,128]{2,1,0:T(8,128)(2,1)} all-to-all(bf16[16,64,128]{2,1,0:T(8,128)(2,1)} %get-tuple-element.144), channel_id=1, replica_groups=mesh['inst'=32,'tp'=16] {'tp'}, dimensions={0} | all-to-all | bytes 524288 | tf_op jit(solution)/shard_map/all_to_all | solution.py:521
  89.5 2.0 %finish.1 = (bf16[8,64,128]{2,1,0:T(8,128)(2,1)}, bf16[3,512]{1,0:T(4,128)(2,1)}, bf16[3,512]{1,0:T(4,128)(2,1)}) custom-call(bf16[16,64,128]{2,1,0:T(8,128)(2,1)} %all_to_all.10.recv, f32[8,512]{1,0:T(8,128)} %get-tuple-element.145.gated, f32[1,512]{1,0:T(1,128)} %bitcast.5), custom_call_target="tpu_custom_call" | custom-call | tf_op jit(solution)/shard_map/finish/pallas_call | solution.py:406
  91.5 3.4 %all-to-all-start.1 = ((bf16[8,64,128]{2,1,0:T(8,128)(2,1)}), bf16[8,64,128]{2,1,0:T(8,128)(2,1)S(1)}, u32[]{:S(2)}, u32[]{:S(2)}) async-start(bf16[8,64,128]{2,1,0:T(8,128)(2,1)} %get-tuple-element.147), calls=%async_computation.1 | async-start | bytes 262144 | tf_op jit(solution)/shard_map/all_to_all | solution.py:523
  94.8 4.3 %update.1 = f32[3,8,64,256]{3,2,1,0:T(8,128)} custom-call(s32[32,2]{1,0:T(8,128)} %copy.30.mig, bf16[624,128]{1,0:T(8,128)(2,1)} %get-tuple-element.151.swapped, bf16[592,128]{1,0:T(8,128)(2,1)} %get-tuple-element.152.moved, bf16[3,512]{1,0:T(4,128)(2,1)} %x1.5, bf16[3,8]{1,0:T(4,128)(2,1)} %dt1.5, bf16[3,1024]{1,0:T(4,128)(2,1)} %b1.5, f32[1,8]{1,0:T(1,128)} %bitcast.7, ...), custom_call_target="tpu_custom_call" | custom-call | tf_op jit(solution)/shard_map/update/pallas_call | solution.py:480
  99.1 1.8 %all-to-all-done.1.recv = bf16[8,64,128]{2,1,0:T(8,128)(2,1)S(1)} async-done(((bf16[8,64,128]{2,1,0:T(8,128)(2,1)}), bf16[8,64,128]{2,1,0:T(8,128)(2,1)S(1)}, u32[]{:S(2)}, u32[]{:S(2)}) %all-to-all-start.1) | async-done | bytes 131104 | tf_op jit(solution)/shard_map/all_to_all | solution.py:523
  100.9 0.0 copy-start
  100.9 0.7 copy-done
  101.6 1.6 %spread.1 = (bf16[3,8192]{1,0:T(4,128)(2,1)}, bf16[3,8192]{1,0:T(4,128)(2,1)}) custom-call(bf16[8,64,128]{2,1,0:T(8,128)(2,1)} %copy-done), custom_call_target="tpu_custom_call" | custom-call | tf_op jit(solution)/shard_map/spread/pallas_call | solution.py:428
Async XLA Ops:
  5.9 22.2 %collective-permute-start.19 = (bf16[624,128]{1,0:T(8,128)(2,1)S(1)}, bf16[624,128]{1,0:T(8,128)(2,1)}, u32[]{:S(2)}, u32[]{:S(2)}) collective-permute-start(bf16[624,128]{1,0:T(8,128)(2,1)S(1)} %param.19), channel_id=1, source_target_pairs={{0,320},{16,336},{32,352},{48,368},{64,256},{80,272},{96,288},{112... | collective-permute-start | bytes 479240 | tf_op jit(solution)/shard_map/cond/branch_19_fun/ppermute | solution.py:495
  33.8 19.6 %collective-permute-start.50 = (bf16[592,128]{1,0:T(8,128)(2,1)S(1)}, bf16[592,128]{1,0:T(8,128)(2,1)}, u32[]{:S(2)}, u32[]{:S(2)}) collective-permute-start(bf16[592,128]{1,0:T(8,128)(2,1)S(1)} %param.50), channel_id=1, source_target_pairs={{0,320},{16,336},{32,352},{48,368},{64,256},{80,272},{96,288},{112... | collective-permute-start | bytes 454664 | tf_op jit(solution)/shard_map/cond/branch_19_fun/ppermute | solution.py:495
  91.5 9.4 %all-to-all-start.1 = ((bf16[8,64,128]{2,1,0:T(8,128)(2,1)}), bf16[8,64,128]{2,1,0:T(8,128)(2,1)S(1)}, u32[]{:S(2)}, u32[]{:S(2)}) async-start(bf16[8,64,128]{2,1,0:T(8,128)(2,1)} %get-tuple-element.147), calls=%async_computation.1 | async-start | bytes 262144 | tf_op jit(solution)/shard_map/all_to_all | solution.py:523
  100.9 0.7 copy-start

commit v3 on v2

--- a/solution.py
+++ b/solution.py
@@ -79,9 +79,14 @@
     return jnp.concatenate([ref[first : first + HDIM, :], ref[second : second + HDIM, :]], axis=1)
 
 
+def entry(mig, column, row):
+    mine = jnp.logical_and(iota(mig.shape, 0) == column, iota(mig.shape, 1) == row)
+    return jnp.sum(jnp.where(mine, mig[...], 0).astype(F32)).astype(I32)
+
+
 def slot_of(mig):
     inst = lax.axis_index("inst")
-    return mig[inst, 0] - inst * REQ
+    return entry(mig, 0, inst) - inst * REQ
 
 
 def whole(a):
@@ -96,14 +101,14 @@
     return [pl.BlockSpec(memory_space=pltpu.SMEM)] * n
 
 
-def call(body, out_shape, in_specs, out_specs, scratch=(), grid=(1,), **kw):
+def call(body, out_shape, in_specs, out_specs, scratch=(), grid=(1,), vmem=60, **kw):
     return pl.pallas_call(
         body,
         out_shape=out_shape,
         in_specs=in_specs,
         out_specs=out_specs,
         scratch_shapes=list(scratch),
-        compiler_params=pltpu.CompilerParams(vmem_limit_bytes=60 * 2**20),
+        compiler_params=pltpu.CompilerParams(vmem_limit_bytes=vmem * 2**20),
         grid=grid,
         **kw,
     )
@@ -143,10 +148,11 @@
     return hi, (v - hi.astype(F32)).astype(BF16)
 
 
-def prepare_body(mig, x1, dt1, b1, q2, kv2, x2, z2, dt2, b2, c2, state, out, rows, held, sem):
+def prepare_body(mig, x1, dt1, b1, q2, kv2, x2, z2, dt2, b2, c2, state, out, pairing, rows, held, sem):
     slot = slot_of(mig)
     copy = pltpu.make_async_copy(state.at[slot, :HALF], held, sem)
     copy.start()
+    pairing[0] = entry(mig, 1, 0)
 
     def put(at, v):
         v = v.astype(F32)
@@ -175,9 +181,9 @@
 def prepare(mig, *rest):
     return call(
         prepare_body,
-        like(SWAP + STATE_ROWS, 128),
-        scalars(1) + [whole(a) for a in rest[:-1]] + [pl.BlockSpec(memory_space=pl.ANY)],
-        here(1)[0],
+        (like(SWAP + STATE_ROWS, 128), like(1, dtype=I32)),
+        [whole(mig)] + [whole(a) for a in rest[:-1]] + [pl.BlockSpec(memory_space=pl.ANY)],
+        (here(1)[0], scalars(1)[0]),
         [VMEM((SWAP, 128), F32), VMEM((HALF, HDIM, STATE), F32), pltpu.SemaphoreType.DMA],
         name="prepare",
     )(mig, *rest)
@@ -200,7 +206,7 @@
 
 
 def partial_body(
-    mig, lens, table, swapped, x1, z1, dt1, b1, c1, q1, kv1, state, cache,
+    lens, table, mig, swapped, x1, z1, dt1, b1, c1, q1, kv1, state, cache,
     rate, bias, skip, x2, z2, dt2, b2, c2, q2, kv2,
     blocks, gated, leaving,
     q8, kv16, x8, z8, d8, b8, c8, scr,
@@ -315,7 +321,7 @@
     leaving[:MOVED, :] = scr[...].astype(BF16)
 
 
-def partials(mig, lens, table, swapped, *rest):
+def partials(lens, table, mig, swapped, *rest):
     return call(
         partial_body,
         (
@@ -323,7 +329,7 @@
             like(8, COLS, dtype=F32),
             like(MOVED + STATE_ROWS, 128),
         ),
-        scalars(3) + here(1) + [whole(a) for a in rest],
+        scalars(2) + [whole(mig)] + here(1) + [whole(a) for a in rest],
         tuple(here(3)),
         [
             VMEM((8, QHEADS * QDIM), F32),
@@ -336,7 +342,7 @@
             VMEM((MOVED, 128), F32),
         ],
         name="partials",
-    )(mig, lens, table, swapped, *rest)
+    )(lens, table, mig, swapped, *rest)
 
 
 def insert_body(mig, blocks, gated, moved, out, gated_out):
@@ -370,7 +376,7 @@
     return call(
         insert_body,
         (like(2 * KVHEADS, QPK * 8, QDIM), like(8, COLS, dtype=F32)),
-        scalars(1) + here(3),
+        [whole(mig)] + here(3),
         tuple(here(2)),
         name="insert",
     )(mig, blocks, gated, moved)
@@ -431,6 +437,7 @@
         here(1),
         tuple(here(2)),
         [VMEM((8, n), F32)],
+        vmem=8,
         name="spread",
     )(recv)
 
@@ -480,7 +487,7 @@
     return call(
         update_body,
         like(*state.shape, dtype=F32),
-        scalars(1) + here(2) + [whole(a) for a in rest[:-1]] + [block],
+        [whole(mig)] + here(2) + [whole(a) for a in rest[:-1]] + [block],
         block,
         [VMEM((8, COLS), F32), VMEM((8, 128), F32), VMEM((8, STATE), F32)],
         grid=(REQ,),
@@ -501,18 +508,19 @@
     x_two, z_two, dt_two, b_two, c_two, q_two, kv_two,
 ):
     rate, bias, skip, gain = decay_rate[None], dt_bias[None], skip_gain[None], norm_gain[None]
-    which = migration[0, 1] - 1
+    migration = migration.T
 
     def by_partner(body, *operands):
         ways = range(1, lax.axis_size("inst"))
-        return lax.switch(which, [functools.partial(body, m) for m in ways], *operands)
-
-    payload = prepare(
+        return lax.switch(pairing - 1, [functools.partial(body, m) for m in ways], *operands)
+
+    payload, pairing = prepare(
         migration, x_one, dt_one, b_one, q_two, kv_two, x_two, z_two, dt_two, b_two, c_two, state
     )
+    pairing = pairing[0]
     swapped = by_partner(swap, payload)
     blocks, gated, leaving = partials(
-        migration, lengths, page_table, swapped,
+        lengths, page_table, migration, swapped,
         x_one, z_one, dt_one, b_one, c_one, q_one, kv_one, state, cache,
         rate, bias, skip, x_two, z_two, dt_two, b_two, c_two, q_two, kv_two,
     )

time: 104 us -> 103 us (level)
  the two profiles are of different devices: /device:TPU:56 before, /device:TPU:32 now
where the time goes in v3:
time: 103 us; the launch traced here: 102 us
  waiting for transfers between devices  35 us (34%)
  blocking collectives  32.5 us (32%)
  Pallas kernels  17.5 us (17%)
  starting transfers between devices  15.7 us (15%)
  between operations  1.3 us (1%)
    ppermute x2, waiting for transfers between devices, swap(): lax.ppermute(v, 'inst', [(s, s ^ m) for s in range(lax.axis_size('inst'))])  33.5 us
    all_to_all x1, blocking collectives, shards(): recv = lax.all_to_all(blocks, 'tp', 0, 0)  32.5 us
    ppermute x2, starting transfers between devices, swap(): lax.ppermute(v, 'inst', [(s, s ^ m) for s in range(lax.axis_size('inst'))])  12.3 us
    pallas_call x1, Pallas kernels, partials(): call(partial_body, (like(KVHEADS, QPK * 8, QDIM), like(8, COLS, dtype=F32...  5.66 us
    pallas_call x1, Pallas kernels, update(): call(update_body, like(*state.shape, dtype=F32), [whole(mig)] + here(2) +...  4.54 us
    all_to_all x1, starting transfers between devices, shards(): recv = lax.all_to_all(blocks, 'tp', 0, 0, axis_index_groups=PLANE)  3.37 us
    pallas_call x1, Pallas kernels, prepare(): call(prepare_body, (like(SWAP + STATE_ROWS, 128), like(1, dtype=I32)), [w...  2.57 us
  transfers between devices with their start and end apart: 3, of which 3 were waited for; matrix products, arithmetic and copies ran while one was open for 0% of the time, Pallas kernels for 4%

profile of v3, /device:TPU:32, one launch (start us, length us, event | category | flops | bytes accessed | tf_op | source)
XLA Modules:
  0.0 102.0 jit_solution(5030333570130944491)
XLA Ops:
  0.6 2.6 %prepare.1 = (bf16[624,128]{1,0:T(8,128)(2,1)S(1)}, s32[1]{0:T(128)}) custom-call(s32[2,32]{1,0:T(2,128)} %bitcast.6, bf16[3,512]{1,0:T(4,128)(2,1)} %x1.5, bf16[3,8]{1,0:T(4,128)(2,1)} %dt1.5, bf16[3,1024]{1,0:T(4,128)(2,1)} %b1.5, bf16[3,8192]{1,0:T(4,128)(2,1)} %q2.3, bf16[3,2048]{1,0:T(4,128)(2,1)} %kv2.3, bf16[3,512]{1,0:T(4,128)(2,1)} %x2.5, ...), custom_call_target="tpu_custom_call" | custom-call | tf_op jit(solution)/shard_map/prepare/pallas_call | solution.py:182
  3.9 24.7 %conditional.2 = (bf16[624,128]{1,0:T(8,128)(2,1)}) conditional(s32[]{:T(128)} %bitcast.1, bf16[624,128]{1,0:T(8,128)(2,1)S(1)} %get-tuple-element.144, bf16[624,128]{1,0:T(8,128)(2,1)S(1)} %get-tuple-element.144, bf16[624,128]{1,0:T(8,128)(2,1)S(1)} %get-tuple-element.144, ...), branch_computations={%region_0.0_spmd, %region_1.0_spmd, %region_2.0_spmd, %region_3.0_... | conditional | bytes 639024 | solution.py:515
  3.9 10.2 %collective-permute-start.22 = (bf16[624,128]{1,0:T(8,128)(2,1)S(1)}, bf16[624,128]{1,0:T(8,128)(2,1)}, u32[]{:S(2)}, u32[]{:S(2)}) collective-permute-start(bf16[624,128]{1,0:T(8,128)(2,1)S(1)} %param.22), channel_id=1, source_target_pairs={{0,368},{16,352},{32,336},{48,320},{64,304},{80,288},{96,272},{112... | collective-permute-start | bytes 479240 | tf_op jit(solution)/shard_map/cond/branch_22_fun/ppermute | solution.py:502
  14.1 14.5 %collective-permute-done.22 = bf16[624,128]{1,0:T(8,128)(2,1)} collective-permute-done((bf16[624,128]{1,0:T(8,128)(2,1)S(1)}, bf16[624,128]{1,0:T(8,128)(2,1)}, u32[]{:S(2)}, u32[]{:S(2)}) %collective-permute-start.22) | collective-permute-done | bytes 159776 | tf_op jit(solution)/shard_map/cond/branch_22_fun/ppermute | solution.py:502
  28.6 5.7 %partials.1 = (bf16[8,64,128]{2,1,0:T(8,128)(2,1)}, f32[8,512]{1,0:T(8,128)}, bf16[592,128]{1,0:T(8,128)(2,1)S(1)}) custom-call(s32[96]{0:T(128)} %lens.1, s32[3,4]{1,0:T(4,128)} %table.1, s32[2,32]{1,0:T(2,128)} %bitcast.7, bf16[624,128]{1,0:T(8,128)(2,1)} %get-tuple-element.155.swapped, bf16[3,512]{1,0:T(4,128)(2,1)} %x1.5, bf16[3,512]{1,0:T(4,128)(2,1)} %z1.1, ...), custom_call_target="tpu_custom_call" | custom-call | tf_op jit(solution)/shard_map/partials/pallas_call | solution.py:325
  34.2 21.2 %conditional.3 = (bf16[592,128]{1,0:T(8,128)(2,1)}) conditional(s32[]{:T(128)} %bitcast.1, bf16[592,128]{1,0:T(8,128)(2,1)S(1)} %get-tuple-element.147, bf16[592,128]{1,0:T(8,128)(2,1)S(1)} %get-tuple-element.147, bf16[592,128]{1,0:T(8,128)(2,1)S(1)} %get-tuple-element.147, ...), branch_computations={%region_31.0_spmd, %region_32.0_spmd, %region_33.0_spmd, %region_3... | conditional | bytes 606256 | solution.py:515
  34.3 2.1 %collective-permute-start.53 = (bf16[592,128]{1,0:T(8,128)(2,1)S(1)}, bf16[592,128]{1,0:T(8,128)(2,1)}, u32[]{:S(2)}, u32[]{:S(2)}) collective-permute-start(bf16[592,128]{1,0:T(8,128)(2,1)S(1)} %param.53), channel_id=1, source_target_pairs={{0,368},{16,352},{32,336},{48,320},{64,304},{80,288},{96,272},{112... | collective-permute-start | bytes 454664 | tf_op jit(solution)/shard_map/cond/branch_22_fun/ppermute | solution.py:502
  36.4 19.0 %collective-permute-done.53 = bf16[592,128]{1,0:T(8,128)(2,1)} collective-permute-done((bf16[592,128]{1,0:T(8,128)(2,1)S(1)}, bf16[592,128]{1,0:T(8,128)(2,1)}, u32[]{:S(2)}, u32[]{:S(2)}) %collective-permute-start.53) | collective-permute-done | bytes 151584 | tf_op jit(solution)/shard_map/cond/branch_22_fun/ppermute | solution.py:502
  55.4 2.0 %insert.1 = (bf16[16,64,128]{2,1,0:T(8,128)(2,1)}, f32[8,512]{1,0:T(8,128)}) custom-call(s32[2,32]{1,0:T(2,128)} %bitcast.8, bf16[8,64,128]{2,1,0:T(8,128)(2,1)} %get-tuple-element.145.blocks, f32[8,512]{1,0:T(8,128)} %get-tuple-element.146.gated, bf16[592,128]{1,0:T(8,128)(2,1)} %get-tuple-element.156.moved), custom_call_target="tpu_custom_call" | custom-call | tf_op jit(solution)/shard_map/insert/pallas_call | solution.py:376
  57.4 32.5 %all_to_all.10.recv = bf16[16,64,128]{2,1,0:T(8,128)(2,1)} all-to-all(bf16[16,64,128]{2,1,0:T(8,128)(2,1)} %get-tuple-element.148), channel_id=1, replica_groups=mesh['inst'=32,'tp'=16] {'tp'}, dimensions={0} | all-to-all | bytes 524288 | tf_op jit(solution)/shard_map/all_to_all | solution.py:529
  89.9 2.0 %finish.1 = (bf16[8,64,128]{2,1,0:T(8,128)(2,1)}, bf16[3,512]{1,0:T(4,128)(2,1)}, bf16[3,512]{1,0:T(4,128)(2,1)}) custom-call(bf16[16,64,128]{2,1,0:T(8,128)(2,1)} %all_to_all.10.recv, f32[8,512]{1,0:T(8,128)} %get-tuple-element.149.gated, f32[1,512]{1,0:T(1,128)} %bitcast.10), custom_call_target="tpu_custom_call" | custom-call | tf_op jit(solution)/shard_map/finish/pallas_call | solution.py:412
  91.8 3.4 %all-to-all-start.1 = ((bf16[8,64,128]{2,1,0:T(8,128)(2,1)}), bf16[8,64,128]{2,1,0:T(8,128)(2,1)S(1)}, u32[]{:S(2)}, u32[]{:S(2)}) async-start(bf16[8,64,128]{2,1,0:T(8,128)(2,1)} %get-tuple-element.151), calls=%async_computation.1 | async-start | bytes 262144 | tf_op jit(solution)/shard_map/all_to_all | solution.py:531
  95.2 4.5 %update.1 = f32[3,8,64,256]{3,2,1,0:T(8,128)} custom-call(s32[2,32]{1,0:T(2,128)} %bitcast.9, bf16[624,128]{1,0:T(8,128)(2,1)} %get-tuple-element.155.swapped, bf16[592,128]{1,0:T(8,128)(2,1)} %get-tuple-element.156.moved, bf16[3,512]{1,0:T(4,128)(2,1)} %x1.5, bf16[3,8]{1,0:T(4,128)(2,1)} %dt1.5, bf16[3,1024]{1,0:T(4,128)(2,1)} %b1.5, f32[1,8]{1,0:T(1,128)} %bitcast.12, ...), custom_call_target="tpu_custom_call" | custom-call | tf_op jit(solution)/shard_map/update/pallas_call | solution.py:487
  99.8 1.5 %all-to-all-done.1.recv = bf16[8,64,128]{2,1,0:T(8,128)(2,1)S(1)} async-done(((bf16[8,64,128]{2,1,0:T(8,128)(2,1)}), bf16[8,64,128]{2,1,0:T(8,128)(2,1)S(1)}, u32[]{:S(2)}, u32[]{:S(2)}) %all-to-all-start.1) | async-done | bytes 131104 | tf_op jit(solution)/shard_map/all_to_all | solution.py:531
  101.3 0.7 spread.1
Async XLA Ops:
  3.9 24.7 %collective-permute-start.22 = (bf16[624,128]{1,0:T(8,128)(2,1)S(1)}, bf16[624,128]{1,0:T(8,128)(2,1)}, u32[]{:S(2)}, u32[]{:S(2)}) collective-permute-start(bf16[624,128]{1,0:T(8,128)(2,1)S(1)} %param.22), channel_id=1, source_target_pairs={{0,368},{16,352},{32,336},{48,320},{64,304},{80,288},{96,272},{112... | collective-permute-start | bytes 479240 | tf_op jit(solution)/shard_map/cond/branch_22_fun/ppermute | solution.py:502
  34.3 21.1 %collective-permute-start.53 = (bf16[592,128]{1,0:T(8,128)(2,1)S(1)}, bf16[592,128]{1,0:T(8,128)(2,1)}, u32[]{:S(2)}, u32[]{:S(2)}) collective-permute-start(bf16[592,128]{1,0:T(8,128)(2,1)S(1)} %param.53), channel_id=1, source_target_pairs={{0,368},{16,352},{32,336},{48,320},{64,304},{80,288},{96,272},{112... | collective-permute-start | bytes 454664 | tf_op jit(solution)/shard_map/cond/branch_22_fun/ppermute | solution.py:502
  91.8 9.4 %all-to-all-start.1 = ((bf16[8,64,128]{2,1,0:T(8,128)(2,1)}), bf16[8,64,128]{2,1,0:T(8,128)(2,1)S(1)}, u32[]{:S(2)}, u32[]{:S(2)}) async-start(bf16[8,64,128]{2,1,0:T(8,128)(2,1)} %get-tuple-element.151), calls=%async_computation.1 | async-start | bytes 262144 | tf_op jit(solution)/shard_map/all_to_all | solution.py:531

commit v4 on v3

--- a/solution.py
+++ b/solution.py
@@ -84,6 +84,18 @@
     return jnp.sum(jnp.where(mine, mig[...], 0).astype(F32)).astype(I32)
 
 
+def pack_rows(v):
+    hi = v.astype(BF16).astype(F32)
+    parts = [t[:, k * 128 : (k + 1) * 128] for t in (hi, v - hi) for k in range(COLS // 128)]
+    return jnp.concatenate(parts, axis=0).astype(BF16)
+
+
+def unpack_rows(v):
+    v = v.astype(F32)
+    v = v[:32] + v[32:]
+    return jnp.concatenate([v[8 * k : 8 * k + 8] for k in range(COLS // 128)], axis=1)
+
+
 def slot_of(mig):
     inst = lax.axis_index("inst")
     return entry(mig, 0, inst) - inst * REQ
@@ -208,7 +220,7 @@
 def partial_body(
     lens, table, mig, swapped, x1, z1, dt1, b1, c1, q1, kv1, state, cache,
     rate, bias, skip, x2, z2, dt2, b2, c2, q2, kv2,
-    blocks, gated, leaving,
+    blocks, leaving,
     q8, kv16, x8, z8, d8, b8, c8, scr,
 ):
     slot = slot_of(mig)
@@ -259,7 +271,7 @@
     row = iota((8, COLS), 0)
     y = decay * jnp.where(row >= 3, first, read) + pushed * same + expand(skip[...], 1) * xx
     g = y * silu(zz)
-    gated[...] = g
+    blocks[KVHEADS] = pack_rows(g)
     g = jnp.sum(jnp.where(row == slot + 3, g, 0.0), axis=0, keepdims=True)
     hi = g.astype(BF16).astype(F32)
     for k in range(4):
@@ -325,12 +337,11 @@
     return call(
         partial_body,
         (
-            like(KVHEADS, QPK * 8, QDIM),
-            like(8, COLS, dtype=F32),
+            like(KVHEADS + 1, QPK * 8, QDIM),
             like(MOVED + STATE_ROWS, 128),
         ),
         scalars(2) + [whole(mig)] + here(1) + [whole(a) for a in rest],
-        tuple(here(3)),
+        tuple(here(2)),
         [
             VMEM((8, QHEADS * QDIM), F32),
             VMEM((EXTRA, KVW), F32),
@@ -345,13 +356,13 @@
     )(lens, table, mig, swapped, *rest)
 
 
-def insert_body(mig, blocks, gated, moved, out, gated_out):
+def insert_body(mig, blocks, moved, out, gated_out):
     slot = slot_of(mig)
     sub = iota((QPK, 8, 128), 1)
     lane = iota((QPK, 8, 128), 2)
     mv = moved[:MOVED, :].astype(F32)
     g = flat(mv[GHI : GHI + 4] + mv[GLO : GLO + 4])
-    g = jnp.where(iota((8, COLS), 0) == slot + 3, g, gated[...])
+    g = jnp.where(iota((8, COLS), 0) == slot + 3, g, unpack_rows(blocks[KVHEADS]))
     gated_out[...] = g
     squares = jnp.sum(g * g, axis=1, keepdims=True)
     sq_row = stats_row(squares[None], sub[:1], lane[:1])
@@ -372,14 +383,15 @@
             out[k // 2 * 4 + z * 2 + k % 2] = v
 
 
-def insert(mig, blocks, gated, moved):
+def insert(mig, blocks, moved):
     return call(
         insert_body,
         (like(2 * KVHEADS, QPK * 8, QDIM), like(8, COLS, dtype=F32)),
-        [whole(mig)] + here(3),
+        [whole(mig)] + here(2),
         tuple(here(2)),
+        vmem=8,
         name="insert",
-    )(mig, blocks, gated, moved)
+    )(mig, blocks, moved)
 
 
 def finish_body(recv, gated, gain, blocks, m1, m2, scr):
@@ -415,6 +427,7 @@
         here(2) + [whole(gain)],
         tuple(here(3)),
         [VMEM((8, COLS), F32)],
+        vmem=8,
         name="finish",
     )(recv, gated, gain)
 
@@ -519,13 +532,13 @@
     )
     pairing = pairing[0]
     swapped = by_partner(swap, payload)
-    blocks, gated, leaving = partials(
+    blocks, leaving = partials(
         lengths, page_table, migration, swapped,
         x_one, z_one, dt_one, b_one, c_one, q_one, kv_one, state, cache,
         rate, bias, skip, x_two, z_two, dt_two, b_two, c_two, q_two, kv_two,
     )
     moved = by_partner(swap, leaving)
-    blocks, gated = insert(migration, blocks, gated, moved)
+    blocks, gated = insert(migration, blocks, moved)
     recv = lax.all_to_all(blocks, "tp", 0, 0)
     blocks, mamba_one, mamba_two = finish(recv, gated, gain)
     recv = lax.all_to_all(blocks, "tp", 0, 0, axis_index_groups=PLANE)

time: 103 us -> 98.2 us (0.953)
  the two profiles are of different devices: /device:TPU:32 before, /device:TPU:48 now
where the time goes in v4:
time: 98.2 us; the launch traced here: 99.4 us
  waiting for transfers between devices  34.6 us (35%)
  blocking collectives  33.1 us (34%)
  Pallas kernels  15.7 us (16%)
  starting transfers between devices  13.7 us (14%)
  between operations  1.33 us (1%)
    ppermute x2, waiting for transfers between devices, swap(): lax.ppermute(v, 'inst', [(s, s ^ m) for s in range(lax.axis_size('inst'))])  33.1 us
    all_to_all x1, blocking collectives, shards(): recv = lax.all_to_all(blocks, 'tp', 0, 0)  33.1 us
    ppermute x2, starting transfers between devices, swap(): lax.ppermute(v, 'inst', [(s, s ^ m) for s in range(lax.axis_size('inst'))])  10.4 us
    pallas_call x1, Pallas kernels, partials(): call(partial_body, (like(KVHEADS + 1, QPK * 8, QDIM), like(MOVED + STATE_...  5.7 us
    pallas_call x1, Pallas kernels, update(): call(update_body, like(*state.shape, dtype=F32), [whole(mig)] + here(2) +...  4.54 us
    all_to_all x1, starting transfers between devices, shards(): recv = lax.all_to_all(blocks, 'tp', 0, 0, axis_index_groups=PLANE)  3.37 us
    pallas_call x1, Pallas kernels, prepare(): call(prepare_body, (like(SWAP + STATE_ROWS, 128), like(1, dtype=I32)), [w...  2.57 us
  transfers between devices with their start and end apart: 3, of which 3 were waited for; matrix products, arithmetic and copies ran while one was open for 0% of the time, Pallas kernels for 5%

profile of v4, /device:TPU:48, one launch (start us, length us, event | category | flops | bytes accessed | tf_op | source)
XLA Modules:
  0.0 99.4 jit_solution(6938111763022329185)
XLA Ops:
  0.6 2.6 %prepare.1 = (bf16[624,128]{1,0:T(8,128)(2,1)S(1)}, s32[1]{0:T(128)}) custom-call(s32[2,32]{1,0:T(2,128)} %bitcast.6, bf16[3,512]{1,0:T(4,128)(2,1)} %x1.5, bf16[3,8]{1,0:T(4,128)(2,1)} %dt1.5, bf16[3,1024]{1,0:T(4,128)(2,1)} %b1.5, bf16[3,8192]{1,0:T(4,128)(2,1)} %q2.3, bf16[3,2048]{1,0:T(4,128)(2,1)} %kv2.3, bf16[3,512]{1,0:T(4,128)(2,1)} %x2.5, ...), custom_call_target="tpu_custom_call" | custom-call | tf_op jit(solution)/shard_map/prepare/pallas_call | solution.py:194
  3.2 0.0 copy-start.1
  3.9 23.0 %conditional.2 = (bf16[624,128]{1,0:T(8,128)(2,1)}) conditional(s32[]{:T(128)} %bitcast.1, bf16[624,128]{1,0:T(8,128)(2,1)S(1)} %get-tuple-element.143, bf16[624,128]{1,0:T(8,128)(2,1)S(1)} %get-tuple-element.143, bf16[624,128]{1,0:T(8,128)(2,1)S(1)} %get-tuple-element.143, ...), branch_computations={%region_0.0_spmd, %region_1.0_spmd, %region_2.0_spmd, %region_3.0_... | conditional | bytes 639024 | solution.py:528
  3.9 8.5 %collective-permute-start.20 = (bf16[624,128]{1,0:T(8,128)(2,1)S(1)}, bf16[624,128]{1,0:T(8,128)(2,1)}, u32[]{:S(2)}, u32[]{:S(2)}) collective-permute-start(bf16[624,128]{1,0:T(8,128)(2,1)S(1)} %param.20), channel_id=1, source_target_pairs={{0,336},{16,320},{32,368},{48,352},{64,272},{80,256},{96,304},{112... | collective-permute-start | bytes 479240 | tf_op jit(solution)/shard_map/cond/branch_20_fun/ppermute | solution.py:515
  12.4 14.5 %collective-permute-done.20 = bf16[624,128]{1,0:T(8,128)(2,1)} collective-permute-done((bf16[624,128]{1,0:T(8,128)(2,1)S(1)}, bf16[624,128]{1,0:T(8,128)(2,1)}, u32[]{:S(2)}, u32[]{:S(2)}) %collective-permute-start.20) | collective-permute-done | bytes 159776 | tf_op jit(solution)/shard_map/cond/branch_20_fun/ppermute | solution.py:515
  26.9 0.0 copy-start.2
  26.9 5.7 %partials.1 = (bf16[9,64,128]{2,1,0:T(8,128)(2,1)}, bf16[592,128]{1,0:T(8,128)(2,1)S(1)}) custom-call(s32[96]{0:T(128)} %lens.1, s32[3,4]{1,0:T(4,128)} %table.1, s32[2,32]{1,0:T(2,128)} %bitcast.7, bf16[624,128]{1,0:T(8,128)(2,1)} %get-tuple-element.153.swapped, bf16[3,512]{1,0:T(4,128)(2,1)} %x1.5, bf16[3,512]{1,0:T(4,128)(2,1)} %z1.1, bf16[3,8]{1,0:T(4,128)(2,1)} %dt1.5, ...), custom_call_target="tpu_custom_call" | custom-call | tf_op jit(solution)/shard_map/partials/pallas_call | solution.py:337
  32.6 20.5 %conditional.3 = (bf16[592,128]{1,0:T(8,128)(2,1)}) conditional(s32[]{:T(128)} %bitcast.1, bf16[592,128]{1,0:T(8,128)(2,1)S(1)} %get-tuple-element.145, bf16[592,128]{1,0:T(8,128)(2,1)S(1)} %get-tuple-element.145, bf16[592,128]{1,0:T(8,128)(2,1)S(1)} %get-tuple-element.145, ...), branch_computations={%region_31.0_spmd, %region_32.0_spmd, %region_33.0_spmd, %region_3... | conditional | bytes 606256 | solution.py:528
  32.6 1.9 %collective-permute-start.51 = (bf16[592,128]{1,0:T(8,128)(2,1)S(1)}, bf16[592,128]{1,0:T(8,128)(2,1)}, u32[]{:S(2)}, u32[]{:S(2)}) collective-permute-start(bf16[592,128]{1,0:T(8,128)(2,1)S(1)} %param.51), channel_id=1, source_target_pairs={{0,336},{16,320},{32,368},{48,352},{64,272},{80,256},{96,304},{112... | collective-permute-start | bytes 454664 | tf_op jit(solution)/shard_map/cond/branch_20_fun/ppermute | solution.py:515
  34.5 18.6 %collective-permute-done.51 = bf16[592,128]{1,0:T(8,128)(2,1)} collective-permute-done((bf16[592,128]{1,0:T(8,128)(2,1)S(1)}, bf16[592,128]{1,0:T(8,128)(2,1)}, u32[]{:S(2)}, u32[]{:S(2)}) %collective-permute-start.51) | collective-permute-done | bytes 151584 | tf_op jit(solution)/shard_map/cond/branch_20_fun/ppermute | solution.py:515
  53.1 0.0 copy-done.1
  53.1 0.0 copy-start
  53.1 0.9 copy-done
  54.0 1.2 %insert.1 = (bf16[16,64,128]{2,1,0:T(8,128)(2,1)S(1)}, f32[8,512]{1,0:T(8,128)S(1)}) custom-call(s32[2,32]{1,0:T(2,128)S(1)} %bitcast.9, bf16[9,64,128]{2,1,0:T(8,128)(2,1)S(1)} %copy-done, bf16[592,128]{1,0:T(8,128)(2,1)} %get-tuple-element.154.moved), custom_call_target="tpu_custom_call" | custom-call | tf_op jit(solution)/shard_map/insert/pallas_call | solution.py:387
  55.2 33.1 %all_to_all.10.recv = bf16[16,64,128]{2,1,0:T(8,128)(2,1)S(1)} all-to-all(bf16[16,64,128]{2,1,0:T(8,128)(2,1)S(1)} %get-tuple-element.146), channel_id=1, replica_groups=mesh['inst'=32,'tp'=16] {'tp'}, dimensions={0} | all-to-all | bytes 524288 | tf_op jit(solution)/shard_map/all_to_all | solution.py:542
  88.3 0.0 copy-done.2
  88.3 1.0 finish.1
  89.3 3.4 %all-to-all-start.1 = ((bf16[8,64,128]{2,1,0:T(8,128)(2,1)}), bf16[8,64,128]{2,1,0:T(8,128)(2,1)S(1)}, u32[]{:S(2)}, u32[]{:S(2)}) async-start(bf16[8,64,128]{2,1,0:T(8,128)(2,1)} %get-tuple-element.149), calls=%async_computation.1 | async-start | bytes 262144 | tf_op jit(solution)/shard_map/all_to_all | solution.py:544
  92.6 4.5 %update.1 = f32[3,8,64,256]{3,2,1,0:T(8,128)} custom-call(s32[2,32]{1,0:T(2,128)} %bitcast.8, bf16[624,128]{1,0:T(8,128)(2,1)} %get-tuple-element.153.swapped, bf16[592,128]{1,0:T(8,128)(2,1)} %get-tuple-element.154.moved, bf16[3,512]{1,0:T(4,128)(2,1)} %x1.5, bf16[3,8]{1,0:T(4,128)(2,1)} %dt1.5, bf16[3,1024]{1,0:T(4,128)(2,1)} %b1.5, f32[1,8]{1,0:T(1,128)} %bitcast.12, ...), custom_call_target="tpu_custom_call" | custom-call | tf_op jit(solution)/shard_map/update/pallas_call | solution.py:500
  97.2 1.5 %all-to-all-done.1.recv = bf16[8,64,128]{2,1,0:T(8,128)(2,1)S(1)} async-done(((bf16[8,64,128]{2,1,0:T(8,128)(2,1)}), bf16[8,64,128]{2,1,0:T(8,128)(2,1)S(1)}, u32[]{:S(2)}, u32[]{:S(2)}) %all-to-all-start.1) | async-done | bytes 131104 | tf_op jit(solution)/shard_map/all_to_all | solution.py:544
  98.7 0.7 spread.1
Async XLA Ops:
  3.2 49.9 %copy-start.1 = (s32[32,2]{0,1:T(2,128)S(1)}, s32[32,2]{0,1:T(2,128)}, u32[]{:S(2)}) copy-start(s32[32,2]{0,1:T(2,128)} %param.96) | copy-start | bytes 772
  3.9 22.9 %collective-permute-start.20 = (bf16[624,128]{1,0:T(8,128)(2,1)S(1)}, bf16[624,128]{1,0:T(8,128)(2,1)}, u32[]{:S(2)}, u32[]{:S(2)}) collective-permute-start(bf16[624,128]{1,0:T(8,128)(2,1)S(1)} %param.20), channel_id=1, source_target_pairs={{0,336},{16,320},{32,368},{48,352},{64,272},{80,256},{96,304},{112... | collective-permute-start | bytes 479240 | tf_op jit(solution)/shard_map/cond/branch_20_fun/ppermute | solution.py:515
  26.9 61.4 %copy-start.2 = (f32[512]{0:T(512)S(1)}, f32[512]{0:T(512)}, u32[]{:S(2)}) copy-start(f32[512]{0:T(512)} %param.100) | copy-start | bytes 6148
  32.6 20.5 %collective-permute-start.51 = (bf16[592,128]{1,0:T(8,128)(2,1)S(1)}, bf16[592,128]{1,0:T(8,128)(2,1)}, u32[]{:S(2)}, u32[]{:S(2)}) collective-permute-start(bf16[592,128]{1,0:T(8,128)(2,1)S(1)} %param.51), channel_id=1, source_target_pairs={{0,336},{16,320},{32,368},{48,352},{64,272},{80,256},{96,304},{112... | collective-permute-start | bytes 454664 | tf_op jit(solution)/shard_map/cond/branch_20_fun/ppermute | solution.py:515
  53.1 0.9 copy-start
  89.3 9.4 %all-to-all-start.1 = ((bf16[8,64,128]{2,1,0:T(8,128)(2,1)}), bf16[8,64,128]{2,1,0:T(8,128)(2,1)S(1)}, u32[]{:S(2)}, u32[]{:S(2)}) async-start(bf16[8,64,128]{2,1,0:T(8,128)(2,1)} %get-tuple-element.149), calls=%async_computation.1 | async-start | bytes 262144 | tf_op jit(solution)/shard_map/all_to_all | solution.py:544
